TPU v7x, 32 devices: a whole 2x2x4 slice. The times are simulated.
32 devices in a mesh: dp: 2 (over x), fsdp: 16 (over z, y, core).
Axes of the slice: x: 2, y: 2, z: 4, core: 2. Of those that a mesh axis runs over, the one named last changes fastest.
Arguments:
- tokens: bfloat16 [81920, 512], P(('dp', 'fsdp')), may hold values from -6 to 6
- positions: bfloat16 [64, 512], P(None, 'fsdp'), may hold values from -4 to 4
- norm_one_gain: bfloat16 [512], P('fsdp'), may hold values from 0.5 to 1.5
- norm_one_bias: bfloat16 [512], P('fsdp'), may hold values from -1 to 1
- qkv_weight: bfloat16 [512, 1536], P('fsdp'), may hold values from -0.25 to 0.25
- out_weight: bfloat16 [512, 512], P('fsdp'), may hold values from -0.75 to 0.75
- norm_two_gain: bfloat16 [512], P('fsdp'), may hold values from 0.5 to 1.5
- norm_two_bias: bfloat16 [512], P('fsdp'), may hold values from -1 to 1
- up_weight: bfloat16 [512, 2048], P('fsdp'), may hold values from -0.25 to 0.25
- up_bias: bfloat16 [2048], P('fsdp'), may hold values from -1.5 to 1.5
- down_weight: bfloat16 [2048, 512], P('fsdp'), may hold values from -0.25 to 0.25
- down_bias: bfloat16 [512], P('fsdp'), may hold values from -1.5 to 1.5
- final_gain: bfloat16 [512], P('fsdp'), may hold values from 0.5 to 1.5
- final_bias: bfloat16 [512], P('fsdp'), may hold values from -1 to 1
- actor_weight: bfloat16 [512, 18], P('fsdp'), may hold values from -0.5 to 0.5
- actor_bias: bfloat16 [18], replicated, may hold values from -4 to 4
- actions: int32 [81920], P(('dp', 'fsdp')), may hold values from 0 to 17, as said below
- action_masks: int32 [81920, 18], P(('dp', 'fsdp')), may hold values from 0 to 1
- game_ids: int32 [1280], P(('dp', 'fsdp')), may hold values from 0 to 25
- returns: float32 [81920], P(('dp', 'fsdp')), may hold values from -8 to 8
- values: float32 [81920], P(('dp', 'fsdp')), may hold values from -6 to 6
- running: float32 [2, 26], replicated, may hold values from -2 to 5, as said below
- percentiles: float32 [2, 26], replicated, may hold values from -2 to 5, as said below
Outputs:
- actor_loss: float32 [], replicated
- statistics: float32 [2, 26], replicated
- tokens_grad: float32 [81920, 512], P(('dp', 'fsdp'))
- positions_grad: float32 [64, 512], P(None, 'fsdp')
- norm_one_gain_grad: float32 [512], P('fsdp')
- norm_one_bias_grad: float32 [512], P('fsdp')
- qkv_weight_grad: float32 [512, 1536], P('fsdp')
- out_weight_grad: float32 [512, 512], P('fsdp')
- norm_two_gain_grad: float32 [512], P('fsdp')
- norm_two_bias_grad: float32 [512], P('fsdp')
- up_weight_grad: float32 [512, 2048], P('fsdp')
- up_bias_grad: float32 [2048], P('fsdp')
- down_weight_grad: float32 [2048, 512], P('fsdp')
- down_bias_grad: float32 [512], P('fsdp')
- final_gain_grad: float32 [512], P('fsdp')
- final_bias_grad: float32 [512], P('fsdp')
- actor_weight_grad: float32 [512, 18], P('fsdp')
- actor_bias_grad: float32 [18], replicated
Inputs may be any that keep to these rules, and one draw needn't show every extreme that they name: `actions`: each frame's taken action is allowed by its mask, and slot 0 is allowed in every frame. `running`: row 1 exceeds row 0 in every game. `percentiles`: row 1 exceeds row 0 in every game.
All inputs are finite; a program needn't handle non-finite values.
Results may differ from a plain program's by a relative error of at most 0.014.
Values may be sent and summed in bfloat16 or wider, within the bound.
A program may use at most 192 MiB of HBM per device.

v0:
```python
import math

import jax
import jax.numpy as jnp
from jax import lax
from jax.sharding import PartitionSpec as P

HEADS = 8
HEAD = 64
LENGTH = 64
GROUP = 128


MASKED = -1e30
EPSILON = 1e-05
DECAY_RATE = 0.9
ENTROPY_WEIGHT = 0.1


def layer_norm(values, gain, offset):
    centred = values - jnp.mean(values, -1, keepdims=True)
    spread = jnp.mean(centred * centred, -1, keepdims=True)
    return centred * lax.rsqrt(spread + EPSILON) * gain + offset


def norm_back(values, gain, offset, upstream):
    unused, pullback = jax.vjp(layer_norm, values, gain, offset)
    return pullback(upstream)


def gelu_exact(values):
    return jax.nn.gelu(values, approximate=False)


def policy_loss(logits, action_masks, actions, advantage):
    allowed = action_masks > 0
    held = jnp.where(allowed, logits, MASKED)
    highest = jnp.max(held, -1, keepdims=True)
    shifted = held - highest
    summed = jnp.sum(jnp.exp(shifted), -1, keepdims=True)
    log_probs = shifted - jnp.log(summed)
    probabilities = jnp.exp(log_probs)
    entropy = -jnp.sum(jnp.where(allowed, probabilities * log_probs, 0.0), -1)
    slot_ids = lax.broadcasted_iota(jnp.int32, held.shape, 1)
    chosen = jnp.sum(jnp.where(slot_ids == actions[:, None], log_probs, 0.0), -1)
    return jnp.sum(-advantage * chosen - ENTROPY_WEIGHT * entropy)


def outer_sum(left, right):
    return lax.dot_general(
        left, right, (((0,), (0,)), ((), ())), preferred_element_type=jnp.float32
    )


def back_product(upstream, weight):
    return lax.dot_general(
        upstream, weight, (((1,), (1,)), ((), ())), preferred_element_type=jnp.float32
    )


def group_mask():
    row_ids = lax.broadcasted_iota(jnp.int32, (GROUP, GROUP), 0)
    col_ids = lax.broadcasted_iota(jnp.int32, (GROUP, GROUP), 1)
    return (row_ids // LENGTH == col_ids // LENGTH) & (col_ids <= row_ids)


def block_scores(query_rows, key_rows):
    raw_scores = jnp.einsum(
        "gqhd,gkhd->ghqk", query_rows, key_rows, preferred_element_type=jnp.float32
    ) * HEAD ** (-0.5)
    return jnp.where(group_mask(), raw_scores, MASKED)


def attend_block(operands):
    query_rows, key_rows, value_rows = operands
    scores = block_scores(query_rows, key_rows)
    highest = jnp.max(scores, -1, keepdims=True)
    weights = jnp.exp(scores - highest)
    summed = jnp.sum(weights, -1, keepdims=True)
    probs_low = (weights / summed).astype(jnp.bfloat16)
    attended = jnp.einsum(
        "ghqk,gkhd->gqhd", probs_low, value_rows, preferred_element_type=jnp.float32
    )
    return (attended.astype(jnp.bfloat16), (highest + jnp.log(summed))[..., 0])


def attend_back(operands):
    query_rows, key_rows, value_rows, attended_grad, log_totals = operands
    scores = block_scores(query_rows, key_rows)
    softmax_rows = jnp.exp(scores - log_totals[..., None])
    probs_low = softmax_rows.astype(jnp.bfloat16)
    value_grad = jnp.einsum(
        "ghqk,gqhd->gkhd", probs_low, attended_grad, preferred_element_type=jnp.float32
    )
    prob_grad = jnp.einsum(
        "gqhd,gkhd->ghqk", attended_grad, value_rows, preferred_element_type=jnp.float32
    )
    row_terms = jnp.sum(prob_grad * softmax_rows, -1, keepdims=True)
    score_grad = (softmax_rows * (prob_grad - row_terms)).astype(jnp.bfloat16)
    query_grad = jnp.einsum(
        "ghqk,gkhd->gqhd", score_grad, key_rows, preferred_element_type=jnp.float32
    ) * HEAD ** (-0.5)
    key_grad = jnp.einsum(
        "ghqk,gqhd->gkhd", score_grad, query_rows, preferred_element_type=jnp.float32
    ) * HEAD ** (-0.5)
    return (
        query_grad.astype(jnp.bfloat16),
        key_grad.astype(jnp.bfloat16),
        value_grad.astype(jnp.bfloat16),
    )


def on_device(
    tokens,
    positions,
    norm_one_gain,
    norm_one_bias,
    qkv_weight,
    out_weight,
    norm_two_gain,
    norm_two_bias,
    up_weight,
    up_bias,
    down_weight,
    down_bias,
    final_gain,
    final_bias,
    actor_weight,
    actor_bias,
    actions,
    action_masks,
    game_ids,
    returns,
    values,
    running,
    percentiles,
):
    row_count = tokens.shape[0]
    width = tokens.shape[1]
    seq_count = row_count // LENGTH
    dp_count = lax.axis_size("dp")
    fsdp_count = lax.axis_size("fsdp")
    device_count = dp_count * fsdp_count
    seq_total = seq_count * device_count
    token_total = row_count * device_count
    full_positions, gain_one, bias_one, qkv_full, out_full = (
        lax.all_gather(positions, "fsdp", axis=1, tiled=True),
        lax.all_gather(norm_one_gain, "fsdp", axis=0, tiled=True),
        lax.all_gather(norm_one_bias, "fsdp", axis=0, tiled=True),
        lax.all_gather(qkv_weight, "fsdp", axis=0, tiled=True),
        lax.all_gather(out_weight, "fsdp", axis=0, tiled=True),
    )
    (
        gain_two,
        bias_two,
        up_full,
        up_bias_full,
        down_full,
        down_bias_full,
        gain_last,
        bias_last,
        actor_full,
    ) = (
        lax.all_gather(norm_two_gain, "fsdp", axis=0, tiled=True),
        lax.all_gather(norm_two_bias, "fsdp", axis=0, tiled=True),
        lax.all_gather(up_weight, "fsdp", axis=0, tiled=True),
        lax.all_gather(up_bias, "fsdp", axis=0, tiled=True),
        lax.all_gather(down_weight, "fsdp", axis=0, tiled=True),
        lax.all_gather(down_bias, "fsdp", axis=0, tiled=True),
        lax.all_gather(final_gain, "fsdp", axis=0, tiled=True),
        lax.all_gather(final_bias, "fsdp", axis=0, tiled=True),
        lax.all_gather(actor_weight, "fsdp", axis=0, tiled=True),
    )
    start_rows = (
        tokens.astype(jnp.float32).reshape(seq_count, LENGTH, width)
        + full_positions.astype(jnp.float32)
    ).reshape(row_count, width)
    gain_one32 = gain_one.astype(jnp.float32)
    bias_one32 = bias_one.astype(jnp.float32)
    normed_low = layer_norm(start_rows, gain_one32, bias_one32).astype(jnp.bfloat16)
    mixed_rows = jnp.dot(normed_low, qkv_full, preferred_element_type=jnp.float32).astype(
        jnp.bfloat16
    )
    group_count = row_count // GROUP
    block_groups = math.gcd(group_count, max(1, 512 // GROUP))
    block_count = group_count // block_groups
    shaped = mixed_rows.reshape(block_count, block_groups, GROUP, 3, HEADS, HEAD)
    query_rows = shaped[:, :, :, 0]
    key_rows = shaped[:, :, :, 1]
    value_rows = shaped[:, :, :, 2]
    attended, log_totals = lax.map(attend_block, (query_rows, key_rows, value_rows))
    attended = attended.reshape(row_count, width)
    middle = start_rows + jnp.dot(attended, out_full, preferred_element_type=jnp.float32)
    gain_two32 = gain_two.astype(jnp.float32)
    bias_two32 = bias_two.astype(jnp.float32)
    two_low = layer_norm(middle, gain_two32, bias_two32).astype(jnp.bfloat16)
    hidden_in = jnp.dot(two_low, up_full, preferred_element_type=jnp.float32) + up_bias_full.astype(
        jnp.float32
    )
    activated, gelu_pull = jax.vjp(gelu_exact, hidden_in)
    active_low = activated.astype(jnp.bfloat16)
    final_rows = (
        middle
        + jnp.dot(active_low, down_full, preferred_element_type=jnp.float32)
        + down_bias_full.astype(jnp.float32)
    )
    gain_last32 = gain_last.astype(jnp.float32)
    bias_last32 = bias_last.astype(jnp.float32)
    last_low = layer_norm(final_rows, gain_last32, bias_last32).astype(jnp.bfloat16)
    logits = jnp.dot(last_low, actor_full, preferred_element_type=jnp.float32) + actor_bias.astype(
        jnp.float32
    )
    fresh_stats = DECAY_RATE * running + (1.0 - DECAY_RATE) * percentiles
    spread = jnp.maximum(1.0, fresh_stats[1] - fresh_stats[0])
    game_slots = lax.broadcasted_iota(jnp.int32, (seq_count, spread.shape[0]), 1)
    seq_spread = jnp.sum(jnp.where(game_slots == game_ids[:, None], spread[None, :], 0.0), 1)
    advantage = ((returns - values).reshape(seq_count, LENGTH) / seq_spread[:, None]).reshape(
        row_count
    )

    def frame_losses(held_logits):
        return policy_loss(held_logits, action_masks, actions, advantage)

    local_loss, policy_pull = jax.vjp(frame_losses, logits)
    (
        gain_two,
        bias_two,
        up_full,
        up_bias_full,
        down_full,
        down_bias_full,
        gain_last,
        bias_last,
        actor_full,
    ) = (
        lax.all_gather(norm_two_gain, "fsdp", axis=0, tiled=True),
        lax.all_gather(norm_two_bias, "fsdp", axis=0, tiled=True),
        lax.all_gather(up_weight, "fsdp", axis=0, tiled=True),
        lax.all_gather(up_bias, "fsdp", axis=0, tiled=True),
        lax.all_gather(down_weight, "fsdp", axis=0, tiled=True),
        lax.all_gather(down_bias, "fsdp", axis=0, tiled=True),
        lax.all_gather(final_gain, "fsdp", axis=0, tiled=True),
        lax.all_gather(final_bias, "fsdp", axis=0, tiled=True),
        lax.all_gather(actor_weight, "fsdp", axis=0, tiled=True),
    )
    cot_scale = jnp.asarray(seq_total, jnp.float32) / token_total
    logit_grad = policy_pull(cot_scale)[0].astype(jnp.bfloat16)
    actor_bias_grad = jnp.sum(logit_grad.astype(jnp.float32), 0)
    actor_grad = outer_sum(last_low, logit_grad)
    last_in = back_product(logit_grad, actor_full)
    final_grad, last_gain_grad, last_bias_grad = norm_back(
        final_rows, gain_last32, bias_last32, last_in
    )
    down_in = final_grad.astype(jnp.bfloat16)
    down_bias_grad = jnp.sum(final_grad, 0)
    down_grad = outer_sum(active_low, down_in)
    active_grad = back_product(down_in, down_full)
    hidden_grad = gelu_pull(active_grad)[0].astype(jnp.bfloat16)
    up_bias_grad = jnp.sum(hidden_grad.astype(jnp.float32), 0)
    up_grad = outer_sum(two_low, hidden_grad)
    two_in = back_product(hidden_grad, up_full)
    middle_back, two_gain_grad, two_bias_grad = norm_back(middle, gain_two32, bias_two32, two_in)
    middle_grad = final_grad + middle_back
    (
        two_gain_part,
        two_bias_part,
        up_part,
        up_bias_part,
        down_part,
        down_bias_part,
        last_gain_part,
        last_bias_part,
        actor_part,
    ) = (
        lax.psum_scatter(two_gain_grad, "fsdp", scatter_dimension=0, tiled=True),
        lax.psum_scatter(two_bias_grad, "fsdp", scatter_dimension=0, tiled=True),
        lax.psum_scatter(up_grad, "fsdp", scatter_dimension=0, tiled=True),
        lax.psum_scatter(up_bias_grad, "fsdp", scatter_dimension=0, tiled=True),
        lax.psum_scatter(down_grad, "fsdp", scatter_dimension=0, tiled=True),
        lax.psum_scatter(down_bias_grad, "fsdp", scatter_dimension=0, tiled=True),
        lax.psum_scatter(last_gain_grad, "fsdp", scatter_dimension=0, tiled=True),
        lax.psum_scatter(last_bias_grad, "fsdp", scatter_dimension=0, tiled=True),
        lax.psum_scatter(actor_grad, "fsdp", scatter_dimension=0, tiled=True),
    )
    full_positions, gain_one, bias_one, qkv_full, out_full = (
        lax.all_gather(positions, "fsdp", axis=1, tiled=True),
        lax.all_gather(norm_one_gain, "fsdp", axis=0, tiled=True),
        lax.all_gather(norm_one_bias, "fsdp", axis=0, tiled=True),
        lax.all_gather(qkv_weight, "fsdp", axis=0, tiled=True),
        lax.all_gather(out_weight, "fsdp", axis=0, tiled=True),
    )
    middle_low = middle_grad.astype(jnp.bfloat16)
    out_grad = outer_sum(attended, middle_low)
    attended_grad = back_product(middle_low, out_full).astype(jnp.bfloat16)
    attended_grad = attended_grad.reshape(block_count, block_groups, GROUP, HEADS, HEAD)
    query_grad, key_grad, value_grad = lax.map(
        attend_back, (query_rows, key_rows, value_rows, attended_grad, log_totals)
    )
    mixed_grad = jnp.stack([query_grad, key_grad, value_grad], 3).reshape(row_count, 3 * width)
    qkv_grad = outer_sum(normed_low, mixed_grad)
    one_in = back_product(mixed_grad, qkv_full)
    start_back, one_gain_grad, one_bias_grad = norm_back(start_rows, gain_one32, bias_one32, one_in)
    start_grad = middle_grad + start_back
    positions_grad = jnp.sum(start_grad.reshape(seq_count, LENGTH, width), 0)
    positions_part, one_gain_part, one_bias_part, qkv_part, out_part = (
        lax.psum_scatter(positions_grad, "fsdp", scatter_dimension=1, tiled=True),
        lax.psum_scatter(one_gain_grad, "fsdp", scatter_dimension=0, tiled=True),
        lax.psum_scatter(one_bias_grad, "fsdp", scatter_dimension=0, tiled=True),
        lax.psum_scatter(qkv_grad, "fsdp", scatter_dimension=0, tiled=True),
        lax.psum_scatter(out_grad, "fsdp", scatter_dimension=0, tiled=True),
    )
    (
        positions_part,
        one_gain_part,
        one_bias_part,
        qkv_part,
        out_part,
        two_gain_part,
        two_bias_part,
        up_part,
        up_bias_part,
        down_part,
        down_bias_part,
        last_gain_part,
        last_bias_part,
        actor_part,
    ) = (
        lax.psum(positions_part.astype(jnp.bfloat16), "dp").astype(jnp.float32),
        lax.psum(one_gain_part.astype(jnp.bfloat16), "dp").astype(jnp.float32),
        lax.psum(one_bias_part.astype(jnp.bfloat16), "dp").astype(jnp.float32),
        lax.psum(qkv_part.astype(jnp.bfloat16), "dp").astype(jnp.float32),
        lax.psum(out_part.astype(jnp.bfloat16), "dp").astype(jnp.float32),
        lax.psum(two_gain_part.astype(jnp.bfloat16), "dp").astype(jnp.float32),
        lax.psum(two_bias_part.astype(jnp.bfloat16), "dp").astype(jnp.float32),
        lax.psum(up_part.astype(jnp.bfloat16), "dp").astype(jnp.float32),
        lax.psum(up_bias_part.astype(jnp.bfloat16), "dp").astype(jnp.float32),
        lax.psum(down_part.astype(jnp.bfloat16), "dp").astype(jnp.float32),
        lax.psum(down_bias_part.astype(jnp.bfloat16), "dp").astype(jnp.float32),
        lax.psum(last_gain_part.astype(jnp.bfloat16), "dp").astype(jnp.float32),
        lax.psum(last_bias_part.astype(jnp.bfloat16), "dp").astype(jnp.float32),
        lax.psum(actor_part.astype(jnp.bfloat16), "dp").astype(jnp.float32),
    )
    loss_total, actor_bias_total = lax.psum((local_loss, actor_bias_grad), ("dp", "fsdp"))
    actor_loss = loss_total / token_total
    return (
        actor_loss,
        fresh_stats,
        start_grad,
        positions_part,
        one_gain_part,
        one_bias_part,
        qkv_part,
        out_part,
        two_gain_part,
        two_bias_part,
        up_part,
        up_bias_part,
        down_part,
        down_bias_part,
        last_gain_part,
        last_bias_part,
        actor_part,
        actor_bias_total,
    )


def solution(mesh):
    in_specs = (
        P(("dp", "fsdp"), None),
        P(None, "fsdp"),
        P("fsdp"),
        P("fsdp"),
        P("fsdp", None),
        P("fsdp", None),
        P("fsdp"),
        P("fsdp"),
        P("fsdp", None),
        P("fsdp"),
        P("fsdp", None),
        P("fsdp"),
        P("fsdp"),
        P("fsdp"),
        P("fsdp", None),
        P(),
        P(("dp", "fsdp")),
        P(("dp", "fsdp"), None),
        P(("dp", "fsdp")),
        P(("dp", "fsdp")),
        P(("dp", "fsdp")),
        P(),
        P(),
    )
    out_specs = (
        P(),
        P(),
        P(("dp", "fsdp"), None),
        P(None, "fsdp"),
        P("fsdp"),
        P("fsdp"),
        P("fsdp", None),
        P("fsdp", None),
        P("fsdp"),
        P("fsdp"),
        P("fsdp", None),
        P("fsdp"),
        P("fsdp", None),
        P("fsdp"),
        P("fsdp"),
        P("fsdp"),
        P("fsdp", None),
        P(),
    )
    return jax.shard_map(
        on_device, mesh=mesh, in_specs=in_specs, out_specs=out_specs, check_vma=False
    )
```

profile of v0, /device:TPU:0, one launch (start us, length us, event | category | flops | bytes accessed | tf_op | source)
XLA Modules:
  0.0 897.4 jit_solution(18364769007911549675)
XLA Ops:
  18.7 35.7 %all-reduce.17 = (bf16[512]{0:T(512)(128)(2,1)S(1)}, bf16[512]{0:T(512)(128)(2,1)S(1)}, bf16[512]{0:T(512)(128)(2,1)S(1)}, bf16[512]{0:T(512)(128)(2,1)S(1)}, bf...) all-reduce(bf16[512]{0:T(512)(128)(2,1)S(1)} %dynamic-update-slice., ...), channel_id=1, replica_groups=mesh['dp'=2,'fsdp'=16] {'fsdp'}, use_global_device_ids=true, to_apply=%add.1 | all-reduce | flops 3584 | bytes 14336
  55.0 17.8 %all_gather.47 = bf16[64,512]{0,1:T(8,128)(2,1)S(1)} all-gather(bf16[64,32]{0,1:T(8,128)(2,1)} %param.28), channel_id=1, replica_groups=mesh['dp'=2,'fsdp'=16] {'fsdp'}, dimensions={1}, use_global_device_ids=true | all-gather | bytes 69632 | tf_op jit(solution)/shard_map/all_gather | solution.py:147
  76.5 21.6 %all_gather.51 = bf16[512,512]{1,0:T(8,128)(2,1)S(1)} all-gather(bf16[32,512]{1,0:T(8,128)(2,1)S(1)} %copy-done.36), channel_id=1, replica_groups=mesh['dp'=2,'fsdp'=16] {'fsdp'}, dimensions={0}, use_global_device_ids=true | all-gather | bytes 557056 | tf_op jit(solution)/shard_map/all_gather | solution.py:151
  98.1 17.3 %all-gather = bf16[16,1,128]{2,1,0:T(2,128)(2,1)S(1)} all-gather(bf16[1,1,128]{2,1,0:T(2,128)(2,1)S(1)} %bitcast.185), channel_id=1, replica_groups=mesh['dp'=2,'fsdp'=16] {'fsdp'}, dimensions={0}, use_global_device_ids=true | all-gather | bytes 4352 | tf_op jit(solution)/shard_map/all_gather | solution.py:167
  116.6 19.2 %all-gather.1 = bf16[16,32,18]{1,2,0:T(8,128)(2,1)S(1)} all-gather(bf16[1,32,18]{1,2,0:T(8,128)(2,1)S(1)} %bitcast.184), channel_id=1, replica_groups=mesh['dp'=2,'fsdp'=16] {'fsdp'}, dimensions={0}, use_global_device_ids=true | all-gather | bytes 19584 | tf_op jit(solution)/shard_map/all_gather | solution.py:172
  140.6 9.6 %convolution_convert_fusion.2 = bf16[2560,1536]{1,0:T(8,128)(2,1)} fusion(bf16[2560,512]{1,0:T(8,128)(2,1)} %add_convert_fusion.3, bf16[512,1536]{1,0:T(8,128)(2,1)} %all-gather.6.cloned.1.call-done), kind=kOutput, calls=%fused_computation.91 | convolution fusion | flops 4030464000 | bytes 12058624 | tf_op jit(solution)/shard_map/dot_general | solution.py:181
  150.3 10.9 %copy.144 = bf16[2560,1536]{0,1:T(8,128)(2,1)} copy(bf16[2560,1536]{1,0:T(8,128)(2,1)} %convolution_convert_fusion.2) | data formatting | bytes 15728640 | tf_op jit(solution)/shard_map/convert_element_type | solution.py:181
  161.2 14.2 %reshape.208 = bf16[5,4,128,3,8,64]{2,1,0,5,4,3:T(4,128)(2,1)} reshape(bf16[2560,1536]{0,1:T(8,128)(2,1)} %copy.144) | data formatting | bytes 15728640 | tf_op jit(solution)/shard_map/reshape | solution.py:187
  175.4 6.1 slice_bitcast_fusion
  188.2 30.0 %while.32 = (s32[]{:T(128)}, bf16[5,4,128,8,64]{2,1,0,4,3:T(4,128)(2,1)}, f32[5,4,8,128]{3,2,1,0:T(8,128)}, bf16[5,4,128,8,64]{2,4,3,1,0:T(8,128)(2,1)}, bf16[5,...) while((s32[]{:T(128)}, bf16[5,4,128,8,64]{2,1,0,4,3:T(4,128)(2,1)}, ...), condition=%wide.region_6.7_spmd, body=%wide.region_3.6_spmd.sunk | while | flops 140850048 | bytes 9637217 | solution.py:191
  218.2 5.5 reshape.209
  231.2 55.2 %multiply_convert_fusion.1 = (bf16[2560,2048]{1,0:T(8,128)(2,1)}, f32[2560,2048]{1,0:T(8,128)}, f32[2560,2048]{1,0:T(8,128)}) fusion(f32[2048]{0:T(1024)S(1)} %bitcast.182, bf16[512,2048]{1,0:T(8,128)(2,1)} %all-gather.8.cloned.1.call-done, f32[2560,512]{1,0:T(8,128)} %copy-done.3, f32[512]{0:T(512)S(1)} %convert_element_type.224, ...), kind=kOutput, calls=%fused_computation.77 | convolution fusion | flops 5721292800 | bytes 59801600 | tf_op jit(solution)/shard_map/dot_general | solution.py:197
  286.4 10.1 %fusion.79 = (f32[2560]{0:T(1024)S(1)}, f32[2560,512]{1,0:T(8,128)S(1)}) fusion(f32[512]{0:T(512)S(1)} %copy-done.44, f32[2560,512]{1,0:T(8,128)} %copy-done.3, bf16[2560,2048]{1,0:T(8,128)(2,1)} %get-tuple-element.535, bf16[2048,512]{1,0:T(8,128)(2,1)} %all-gather.10.cloned.1.call-done), kind=kOutput, calls=%fused_computation.187 | convolution fusion | flops 5372638720 | bytes 23080960 | tf_op jit(solution)/shard_map/dot_general | solution.py:204
  309.2 24.4 %convert_reduce_fusion = (f32[2048]{0:T(1024)S(1)}, bf16[2560,2048]{1,0:T(8,128)(2,1)}) fusion(f32[2560,2048]{1,0:T(8,128)} %get-tuple-element.536, bf16[2048,512]{1,0:T(8,128)(2,1)} %all-gather.10.cloned.1.call-done, f32[2560,512]{1,0:T(8,128)} %get-tuple-element.530, f32[2560]{0:T(1024)S(1)} %negate_multiply_fusion.3, ...), kind=kOutput, calls=%fused_computation.75 | convolution fusion | flops 5460457472 | bytes 59795456 | tf_op jit(solution)/shard_map/dot_general | solution.py:56
  333.6 11.7 %multiply_reduce_fusion.2 = (f32[512]{0:T(512)S(1)}, f32[2560]{0:T(1024)S(1)}, f32[512]{0:T(512)S(1)}, f32[2560,512]{1,0:T(8,128)S(1)}) fusion(f32[2560,512]{1,0:T(8,128)} %copy-done.3, f32[2560]{0:T(1024)S(1)} %fusion.66, f32[2560]{0:T(1024)S(1)} %broadcast_multiply_fusion.2, f32[512]{0:T(512)S(1)} %convert_element_type.223, ...), kind=kOutput, calls=%fused_computation.98 | convolution fusion | flops 5379191296 | bytes 23105536 | tf_op jit(solution)/shard_map/dot_general | solution.py:56
  365.0 56.7 %while.33 = (s32[]{:T(128)}, bf16[5,4,128,8,64]{2,4,3,1,0:T(8,128)(2,1)}, bf16[5,4,128,8,64]{2,4,3,1,0:T(8,128)(2,1)}, bf16[5,4,128,8,64]{2,4,3,1,0:T(8,128)(2,1...) while((s32[]{:T(128)}, ...), condition=%wide.region_26.27_spmd, body=%wide.region_24.26_spmd.sunk | while | flops 341652352 | bytes 21093744 | solution.py:296
  421.7 6.9 pad_maximum_fusion
  428.6 13.5 %copy.155 = bf16[5,4,128,3,8,64]{2,1,0,5,4,3:T(4,128)(2,1)} copy(bf16[5,4,128,3,8,64]{2,5,4,1,0,3:T(8,128)(2,1)} %pad_maximum_fusion) | data formatting | bytes 15728640 | tf_op jit(solution)/shard_map/stack | solution.py:299
  442.1 13.9 %reshape.211 = bf16[2560,1536]{0,1:T(8,128)(2,1)} reshape(bf16[5,4,128,3,8,64]{2,1,0,5,4,3:T(4,128)(2,1)} %copy.155) | data formatting | bytes 15728640 | tf_op jit(solution)/shard_map/reshape | solution.py:299
  456.0 8.3 fusion.81
  464.6 13.8 %fusion.71 = f32[512,2048]{1,0:T(8,128)} fusion(bf16[2560,2048]{1,0:T(8,128)(2,1)} %get-tuple-element.566, f32[2560,512]{1,0:T(8,128)} %copy-done.3, f32[512]{0:T(512)S(1)} %copy-done.43, f32[512]{0:T(512)S(1)} %convert_element_type.223, f32[2560]{0:T(1024)S(1)} %fusion.66, f32[2560]{0:T(1024)S(1)} %broadcast_multiply_fusion.2), kind=kOutput, calls=%fused_computation.180 | convolution fusion | flops 5375262720 | bytes 19947520 | tf_op jit(solution)/shard_map/dot_general | solution.py:50
  478.5 13.3 %fusion.69 = f32[2048,512]{1,0:T(8,128)} fusion(bf16[2560,2048]{1,0:T(8,128)(2,1)} %get-tuple-element.535, f32[2560,512]{1,0:T(8,128)} %get-tuple-element.530, f32[2560]{0:T(1024)S(1)} %negate_multiply_fusion.3), kind=kOutput, calls=%fused_computation.178 | convolution fusion | flops 5371330560 | bytes 19933184 | tf_op jit(solution)/shard_map/dot_general | solution.py:50
  493.6 9.7 %fusion.73 = (f32[512]{0:T(512)S(1)}, f32[2560]{0:T(1024)S(1)}, f32[2560,512]{1,0:T(8,128)S(1)}) fusion(f32[512]{0:T(512)S(1)} %copy-done.31, f32[2560]{0:T(1024)S(1)} %copy-done.18, f32[64,512]{1,0:T(8,128)S(1)} %copy-done.10, bf16[2560,512]{1,0:T(8,128)(2,1)S(1)} %copy-done.1, bf16[2560,1536]{0,1:T(8,128)(2,1)} %reshape.211, ...), kind=kOutput, calls=%fused_computation.182 | convolution fusion | flops 4035703808 | bytes 17457152 | tf_op jit(solution)/shard_map/dot_general | solution.py:56
  510.9 9.0 add_add_fusion.3
  530.7 73.0 %reduce-scatter.15.cloned.1.call-done = f32[32,2048]{1,0:T(8,128)} async-done(((f32[512,2048]{1,0:T(8,128)}), f32[32,2048]{1,0:T(8,128)}) %reduce-scatter.15.cloned.1.call-update) | async-done | bytes 262160 | tf_op jit(solution)/shard_map/reduce_scatter | solution.py:277
  605.3 74.3 %reduce-scatter.17.cloned.1.call-done = f32[128,512]{1,0:T(8,128)} async-done(((f32[2048,512]{1,0:T(8,128)}), f32[128,512]{1,0:T(8,128)}) %reduce-scatter.17.cloned.1.call-update) | async-done | bytes 262160 | tf_op jit(solution)/shard_map/reduce_scatter | solution.py:279
  682.6 39.9 %all-reduce.15 = (f32[]{:T(128)}, f32[18]{0:T(128)}) all-reduce(f32[]{:T(128)} %get-tuple-element.568, f32[18]{0:T(128)S(1)} %copy-done.48), channel_id=1, replica_groups=mesh['dp'=2,'fsdp'=16] {'dp','fsdp'}, use_global_device_ids=true, to_apply=%region_16.17 | all-reduce | flops 19 | bytes 152 | tf_op jit(solution)/shard_map/psum | solution.py:343
  722.5 59.3 %all-reduce.16 = (bf16[512]{0:T(512)(128)(2,1)S(1)}, bf16[512]{0:T(512)(128)(2,1)S(1)}, bf16[512]{0:T(512)(128)(2,1)S(1)}, bf16[512]{0:T(512)(128)(2,1)S(1)}, bf...) all-reduce(f32[512]{0:T(512)S(1)} %get-tuple-element.457, ...), channel_id=3, replica_groups=mesh['dp'=2,'fsdp'=16] {'fsdp'}, use_global_device_ids=true, to_apply=%region_33.34.clone | all-reduce | flops 5632 | bytes 33792
  783.9 12.8 %reduce-scatter.19.cloned.1.call-done = f32[32,64]{1,0:T(8,128)} async-done(((f32[512,64]{1,0:T(8,128)}), f32[32,64]{1,0:T(8,128)}) %reduce-scatter.19.cloned.1.call-update) | async-done | bytes 8208
  797.4 59.3 %reduce-scatter.13.cloned.1.call-done = f32[32,512]{1,0:T(8,128)} async-done(((f32[512,512]{1,0:T(8,128)}), f32[32,512]{1,0:T(8,128)}) %reduce-scatter.13.cloned.1.call-update) | async-done | bytes 65552 | tf_op jit(solution)/shard_map/reduce_scatter | solution.py:310
  857.6 9.2 %all-reduce.18 = (bf16[64,32]{1,0:T(8,128)(2,1)S(1)}, bf16[32]{0:T(256)(128)(2,1)S(1)}, bf16[32]{0:T(256)(128)(2,1)S(1)}, bf16[32,512]{1,0:T(8,128)(2,1)S(1)}, b...) all-reduce(bf16[64,32]{1,0:T(8,128)(2,1)S(1)} %copy.164, ...), channel_id=1, replica_groups=mesh['dp'=2,'fsdp'=16] {'dp'}, use_global_device_ids=true, to_apply=%region_31.32 | all-reduce | flops 19360 | bytes 77440 | tf_op jit(solution)/shard_map/psum | solution.py:328
  872.8 11.3 %all-reduce.22.cloned.1.call-done = (bf16[32,1536]{1,0:T(8,128)(2,1)}, bf16[32,2048]{1,0:T(8,128)(2,1)}, bf16[128,512]{1,0:T(8,128)(2,1)}) async-done(((bf16[32,1536]{1,0:T(8,128)(2,1)}, bf16[32,2048]{1,0:T(8,128)(2,1)}, bf16[128,512]{1,0:T(8,128)(2,1)}), (bf16[32,1536]{1,0:T(8,128)(2,1)}, bf16[32,2048]{1,0:T(8,128)(2,1)}, bf16[128,512]{1,0:T(8,128)(2,1)})) %all-reduce.22.cloned.1.call-update) | async-done | bytes 360464 | tf_op jit(solution)/shard_map/psum | solution.py:331
  (330 shorter events, 191.0 us)
Async XLA Ops:
  7.2 68.1 %copy-start = (bf16[2560,512]{1,0:T(8,128)(2,1)S(1)}, bf16[2560,512]{1,0:T(8,128)(2,1)}, u32[]{:S(2)}) copy-start(bf16[2560,512]{1,0:T(8,128)(2,1)} %param.27) | copy-start | bytes 7864324
  7.2 69.2 %copy-start.36 = (bf16[32,512]{1,0:T(8,128)(2,1)S(1)}, bf16[32,512]{1,0:T(8,128)(2,1)}, u32[]{:S(2)}) copy-start(bf16[32,512]{1,0:T(8,128)(2,1)} %param.32) | copy-start | bytes 98308
  7.2 90.8 %copy-start.49 = (bf16[128]{0:T(256)(128)(2,1)S(1)}, bf16[128]{0:T(256)(128)(2,1)}, u32[]{:S(2)}) copy-start(bf16[128]{0:T(256)(128)(2,1)} %param.36) | copy-start | bytes 772
  7.2 109.4 %copy-start.41 = (bf16[32,18]{0,1:T(8,128)(2,1)S(1)}, bf16[32,18]{0,1:T(8,128)(2,1)}, u32[]{:S(2)}) copy-start(bf16[32,18]{0,1:T(8,128)(2,1)} %param.41) | copy-start | bytes 3460
  7.2 129.3 %copy-start.45 = (f32[2,26]{1,0:T(2,128)S(1)}, f32[2,26]{1,0:T(2,128)}, u32[]{:S(2)}) copy-start(f32[2,26]{1,0:T(2,128)} %param.49) | copy-start | bytes 628
  7.2 129.3 %copy-start.46 = (f32[2,26]{1,0:T(2,128)S(1)}, f32[2,26]{1,0:T(2,128)}, u32[]{:S(2)}) copy-start(f32[2,26]{1,0:T(2,128)} %param.48) | copy-start | bytes 628
  7.3 129.4 %copy-start.52 = (s32[40]{0:T(128)S(1)}, s32[40]{0:T(128)}, u32[]{:S(2)}) copy-start(s32[40]{0:T(128)} %param.45) | copy-start | bytes 484
  7.3 133.4 %all-gather.6.cloned.1.call-start = ((), (), s32[]{:S(2)}) async-start(), calls=%async_computation.6 | async-start | bytes 1671168 | tf_op jit(solution)/shard_map/all_gather | solution.py:150
  8.0 223.2 %all-gather.8.cloned.1.call-start = ((), (), s32[]{:S(2)}) async-start(), calls=%async_computation.7 | async-start | bytes 2228224 | tf_op jit(solution)/shard_map/all_gather | solution.py:166
  8.7 277.6 %all-gather.10.cloned.1.call-start = ((), (), s32[]{:S(2)}) async-start(), calls=%async_computation.8 | async-start | bytes 2228224 | tf_op jit(solution)/shard_map/all_gather | solution.py:168
  9.5 519.6 %reduce-scatter.11.cloned.1.call-start = ((), (), s32[]{:S(2)}) async-start(), calls=%async_computation.9 | async-start | bytes 3342336 | tf_op jit(solution)/shard_map/reduce_scatter | solution.py:309
  55.0 85.1 %copy-start.30 = (f32[512]{0:T(512)}, f32[512]{0:T(512)S(1)}, u32[]{:S(2)}) copy-start(f32[512]{0:T(512)S(1)} %convert_element_type.219) | copy-start | bytes 6148
  72.8 150.8 %copy-start.9 = (f32[64,512]{1,0:T(8,128)}, f32[64,512]{1,0:T(8,128)S(1)}, u32[]{:S(2)}) copy-start(f32[64,512]{1,0:T(8,128)S(1)} %convert_element_type.218) | copy-start | bytes 393220
  75.2 64.8 %copy-start.32 = (f32[2560]{0:T(1024)S(1)}, f32[2560]{0:T(1024)}, u32[]{:S(2)}) copy-start(f32[2560]{0:T(1024)} %param.46) | copy-start | bytes 30724
  75.2 64.8 %copy-start.34 = (f32[2560]{0:T(1024)S(1)}, f32[2560]{0:T(1024)}, u32[]{:S(2)}) copy-start(f32[2560]{0:T(1024)} %param.47) | copy-start | bytes 30724
  75.3 75.0 %copy-start.17 = (f32[2560]{0:T(1024)}, f32[2560]{0:T(1024)S(1)}, u32[]{:S(2)}) copy-start(f32[2560]{0:T(1024)S(1)} %broadcast_multiply_fusion.3) | copy-start | bytes 30724
  76.4 40.2 %copy-start.23 = (f32[2560]{0:T(1024)}, f32[2560]{0:T(1024)S(1)}, u32[]{:S(2)}) copy-start(f32[2560]{0:T(1024)S(1)} %multiply_reduce_fusion.9) | copy-start | bytes 30724
  76.4 73.8 %copy-start.20 = (f32[2560]{0:T(1024)}, f32[2560]{0:T(1024)S(1)}, u32[]{:S(2)}) copy-start(f32[2560]{0:T(1024)S(1)} %fusion.65) | copy-start | bytes 30724
  98.0 125.6 %copy-start.11 = (bf16[512,512]{1,0:T(8,128)(2,1)}, bf16[512,512]{1,0:T(8,128)(2,1)S(1)}, u32[]{:S(2)}) copy-start(bf16[512,512]{1,0:T(8,128)(2,1)S(1)} %all_gather.51) | copy-start | bytes 1572868
  115.4 115.8 %copy-start.42 = (f32[512]{0:T(512)}, f32[512]{0:T(512)S(1)}, u32[]{:S(2)}) copy-start(f32[512]{0:T(512)S(1)} %convert_element_type.224) | copy-start | bytes 6148
  231.2 55.2 %copy-start.44 = (f32[512]{0:T(512)S(1)}, f32[512]{0:T(512)}, u32[]{:S(2)}) copy-start(f32[512]{0:T(512)} %convert_element_type.228) | copy-start | bytes 6148
  309.2 24.4 %copy-start.51 = (bf16[512,2048]{1,0:T(8,128)(2,1)S(1)}, bf16[512,2048]{1,0:T(8,128)(2,1)}, u32[]{:S(2)}) copy-start(bf16[512,2048]{1,0:T(8,128)(2,1)} %all-gather.8.cloned.1.call-done) | copy-start | bytes 6291460
  464.3 139.3 %reduce-scatter.15.cloned.1.call-start = ((), (), s32[]{:S(2)}) async-start(), calls=%async_computation.11 | async-start | bytes 4456448 | tf_op jit(solution)/shard_map/reduce_scatter | solution.py:277
  478.4 201.2 %reduce-scatter.17.cloned.1.call-start = ((), (), s32[]{:S(2)}) async-start(), calls=%async_computation.12 | async-start | bytes 4456448 | tf_op jit(solution)/shard_map/reduce_scatter | solution.py:279
  491.9 14.1 %copy-start.21 = (f32[2560]{0:T(1024)S(1)}, f32[2560]{0:T(1024)}, u32[]{:S(2)}) copy-start(f32[2560]{0:T(1024)} %copy-done.20) | copy-start | bytes 30724
  491.9 291.2 %reduce-scatter.21.cloned.1.call-start = ((), (), s32[]{:S(2)}) async-start(), calls=%async_computation.14 | async-start | bytes 278528
  510.9 285.8 %reduce-scatter.19.cloned.1.call-start = ((), (), s32[]{:S(2)}) async-start(), calls=%async_computation.13 | async-start | bytes 278528
  523.9 158.7 %copy-start.48 = (f32[18]{0:T(128)S(1)}, f32[18]{0:T(128)}, u32[]{:S(2)}) copy-start(f32[18]{0:T(128)} %get-tuple-element.531) | copy-start | bytes 220
  523.9 198.6 %copy-start.38 = (f32[512]{0:T(512)S(1)}, f32[512]{0:T(512)}, u32[]{:S(2)}) copy-start(f32[512]{0:T(512)} %get-tuple-element.453) | copy-start | bytes 6148
  523.9 198.6 %copy-start.39 = (f32[512]{0:T(512)S(1)}, f32[512]{0:T(512)}, u32[]{:S(2)}) copy-start(f32[512]{0:T(512)} %get-tuple-element.459) | copy-start | bytes 6148
  523.9 332.9 %reduce-scatter.13.cloned.1.call-start = ((), (), s32[]{:S(2)}) async-start(), calls=%async_computation.10 | async-start | bytes 1114112 | tf_op jit(solution)/shard_map/reduce_scatter | solution.py:310
  529.0 355.1 %all-reduce.22.cloned.1.call-start = ((), (), s32[]{:S(2)}) async-start(), calls=%async_computation.15 | async-start | bytes 720896 | tf_op jit(solution)/shard_map/psum | solution.py:331
  (31 other events, 162.9 us)
Sparse Core Ops, SparseCore 0:
  10.4 42.6 all-gather.5
  55.2 42.2 all-gather.7
  99.7 40.5 all-gather.9
  464.5 64.1 reduce-scatter.10
  532.4 71.2 reduce-scatter.14
  607.9 71.7 reduce-scatter.16
  683.7 54.4 reduce-scatter.20
  742.2 54.3 reduce-scatter.18
  800.3 56.4 reduce-scatter.12
  859.8 24.2 all-reduce.21
where the time goes:
time: 907 us; the launch traced here: 897 us
  matrix products  239 us (26%)
  waiting for transfers between devices  233 us (26%)
  blocking collectives  220 us (24%)
  local copies, waits for them, and re-layouts  112 us (12%)
  other arithmetic  72.6 us (8%)
  between operations  19.3 us (2%)
    unnamed x2, blocking collectives  95 us
    reduce_scatter x1, waiting for transfers between devices, on_device(): lax.psum_scatter(down_grad, 'fsdp', scatter_dimension=0, tiled=True)  74.3 us
    reduce_scatter x1, waiting for transfers between devices, on_device(): lax.psum_scatter(up_grad, 'fsdp', scatter_dimension=0, tiled=True)  73 us
    reduce_scatter x1, waiting for transfers between devices, on_device(): lax.psum_scatter(out_grad, 'fsdp', scatter_dimension=0, tiled=True)  59.3 us
    dot_general x1, matrix products, on_device(): jnp.dot(two_low, up_full, preferred_element_type=jnp.float32)  55.2 us
    dot_general x5, matrix products, back_product(): lax.dot_general(upstream, weight, (((1,), (1,)), ((), ())), preferred_ele...  50.2 us
    dot_general x4, matrix products, outer_sum(): lax.dot_general(left, right, (((0,), (0,)), ((), ())), preferred_element_...  40.4 us
    psum x1, blocking collectives, on_device(): lax.psum((local_loss, actor_bias_grad), ('dp', 'fsdp'))  39.9 us
  transfers between devices with their start and end apart: 10, of which 5 were waited for; matrix products, arithmetic and copies ran while one was open for 26% of the time, Pallas kernels for 0%

commit v1 on v0

v1 whole, which is shorter than its diff:
```python
import functools
import math
import math

import jax
import jax.numpy as jnp
from jax import lax
from jax.experimental import pallas as pl
from jax.experimental.pallas import tpu as pltpu
from jax.sharding import PartitionSpec as P

HEADS = 8
HEAD = 64
LENGTH = 64
QUAD = 4
WIDE = QUAD * HEAD
MASKED = -1e30
EPSILON = 1e-05
DECAY_RATE = 0.9
ENTROPY_WEIGHT = 0.1
SLOTS = 32
VMEM_BYTES = 63 * 1024 * 1024
BF16 = jnp.bfloat16
F32 = jnp.float32

G1, B1, G2, B2, DB, GL, BL = range(7)
MESH = pl.DeviceIdType.MESH


def dot(left, right, left_dim, right_dim):
    return lax.dot_general(
        left, right, (((left_dim,), (right_dim,)), ((), ())), preferred_element_type=F32
    )


def mean_last(values):
    return jnp.sum(values, -1, keepdims=True) * (1.0 / values.shape[-1])


def normalise(values):
    centred = values - mean_last(values)
    scale = lax.rsqrt(mean_last(centred * centred) + EPSILON)
    return centred * scale, scale


def norm_back(unit, scale, gain, upstream):
    inner = upstream * gain
    return scale * (inner - mean_last(inner) - unit * mean_last(inner * unit))


def fold_rows(values):
    rows, width = values.shape
    return jnp.sum(values.reshape(rows // 8, 8, width), 0)


def gelu_pair(values):
    half = jnp.exp2(values * values * (-0.5 * 1.4426950408889634))
    span = 1.0 + jnp.abs(values) * (0.3275911 * 0.7071067811865476)
    guess = pl.reciprocal(span, approx=True)
    t = guess * (2.0 - span * guess)
    poly = t * (
        0.5 * 0.254829592
        + t
        * (
            0.5 * -0.284496736
            + t * (0.5 * 1.421413741 + t * (0.5 * -1.453152027 + t * (0.5 * 1.061405429)))
        )
    )
    tail = poly * half
    cdf = jnp.where(values < 0.0, tail, 1.0 - tail)
    density = half * 0.3989422804014327
    return values * cdf, cdf + values * density


def pair_masks():
    lane = lax.broadcasted_iota(jnp.int32, (LENGTH, 2 * HEAD), 1)
    first = jnp.where(lane < HEAD, 1.0, 0.0)
    return first.astype(BF16), (1.0 - first).astype(BF16)


def spread_heads(rows, masks):
    zero = jnp.zeros((LENGTH, 2 * HEAD), BF16)
    left, right = rows[:, : 2 * HEAD], rows[:, 2 * HEAD :]
    blocks = [jnp.concatenate([left * mask, zero], 1) for mask in masks]
    blocks += [jnp.concatenate([zero, right * mask], 1) for mask in masks]
    return jnp.concatenate(blocks, 0)


def gather_heads(blocks):
    lane = lax.broadcasted_iota(jnp.int32, (LENGTH, 2 * HEAD), 1)
    pairs = []
    for pair in range(QUAD // 2):
        lanes = slice(pair * 2 * HEAD, (pair + 1) * 2 * HEAD)
        low = 2 * pair * HEAD
        first, second = blocks[low : low + HEAD, lanes], blocks[low + HEAD : low + 2 * HEAD, lanes]
        pairs.append(jnp.where(lane < HEAD, first, second))
    return jnp.concatenate(pairs, 1)


def causal_bias():
    key = lax.broadcasted_iota(jnp.int32, (LENGTH, WIDE), 0)
    query = lax.rem(lax.broadcasted_iota(jnp.int32, (LENGTH, WIDE), 1), HEAD)
    return jnp.where(key <= query, 0.0, MASKED)


LOG2E = 1.4426950408889634
SCORE_SCALE = HEAD ** (-0.5) * LOG2E


def chains(r, i):
    width = r.tokens.shape[1]
    found = []
    for s in range(4):
        row = pl.multiple_of((4 * i + s) * LENGTH, LENGTH)
        for half in range(width // WIDE):
            at = half * WIDE
            columns = [slice(k * width + at, k * width + at + WIDE) for k in range(3)]
            found.append((4 * i + s, pl.ds(row, LENGTH), columns))
    return found


def attend_group(r, i):
    masks, bias = pair_masks(), r.causal[...]
    group = chains(r, i)
    scores = [
        dot(r.qkv[rows, k], spread_heads(r.qkv[rows, q], masks), 1, 1)
        for _, rows, (q, k, _) in group
    ]
    probs = []
    for (seq, _, (q, _, _)), score in zip(group, scores, strict=True):
        score = score * SCORE_SCALE + bias
        highest = jnp.max(score, 0, keepdims=True)
        weights = jnp.exp2(score - highest)
        summed = jnp.sum(weights, 0, keepdims=True)
        probs.append((weights * (1.0 / summed)).astype(BF16))
        r.totals[pl.ds(seq, 1), q] = highest + jnp.log(summed) * LOG2E
    blocks = [
        dot(prob, r.qkv[rows, v], 0, 0) for (_, rows, (_, _, v)), prob in zip(group, probs, strict=True)
    ]
    for (_, rows, (q, _, _)), block in zip(group, blocks, strict=True):
        r.attended[rows, q] = gather_heads(block).astype(BF16)


def attend_back_group(r, i):
    masks, bias = pair_masks(), r.causal[...]
    done = []
    for half in range(2):
        group = chains(r, i)[half::2]
        queries = [spread_heads(r.qkv[rows, q], masks) for _, rows, (q, _, _) in group]
        aboves = [spread_heads(r.attended[rows, q], masks) for _, rows, (q, _, _) in group]
        scores = [
            dot(r.qkv[rows, k], query, 1, 1)
            for (_, rows, (_, k, _)), query in zip(group, queries, strict=True)
        ]
        prob_grads = [
            dot(r.qkv[rows, v], above, 1, 1)
            for (_, rows, (_, _, v)), above in zip(group, aboves, strict=True)
        ]
        probs, score_grads = [], []
        for (seq, _, (q, _, _)), score, pull in zip(group, scores, prob_grads, strict=True):
            prob = jnp.exp2(score * SCORE_SCALE + bias - r.totals[pl.ds(seq, 1), q])
            row_terms = jnp.sum(pull * prob, 0, keepdims=True)
            score_grads.append((prob * (pull - row_terms)).astype(BF16))
            probs.append(prob.astype(BF16))
        value_grads = [dot(prob, above, 1, 0) for prob, above in zip(probs, aboves, strict=True)]
        key_grads = [dot(grad, query, 1, 0) for grad, query in zip(score_grads, queries, strict=True)]
        query_grads = [
            dot(grad, r.qkv[rows, k], 0, 0)
            for (_, rows, (_, k, _)), grad in zip(group, score_grads, strict=True)
        ]
        for (_, rows, (q, k, v)), dq, dk, dv in zip(
            group, query_grads, key_grads, value_grads, strict=True
        ):
            done.append((rows, q, (gather_heads(dq) * HEAD ** (-0.5)).astype(BF16)))
            done.append((rows, k, (dk * HEAD ** (-0.5)).astype(BF16)))
            done.append((rows, v, dv.astype(BF16)))
    for rows, columns, grad in done:
        r.qkv[rows, columns] = grad


def policy(logits, masks, actions, advantage, scale):
    allowed = masks > 0
    held = jnp.where(allowed, logits, MASKED)
    shifted = held - jnp.max(held, 0, keepdims=True)
    weights = jnp.exp(shifted)
    summed = jnp.sum(weights, 0, keepdims=True)
    log_probs = shifted - jnp.log(summed)
    probs = weights * (1.0 / summed)
    plogp = jnp.where(allowed, probs * log_probs, 0.0)
    entropy = -jnp.sum(plogp, 0, keepdims=True)
    slot = lax.broadcasted_iota(jnp.int32, logits.shape, 0)
    taken = slot == actions
    chosen = jnp.sum(jnp.where(taken, log_probs, 0.0), 0, keepdims=True)
    loss = -advantage * chosen - ENTROPY_WEIGHT * entropy
    pull = advantage * (probs - jnp.where(taken, 1.0, 0.0)) + ENTROPY_WEIGHT * (
        plogp + probs * entropy
    )
    return loss, jnp.where(allowed, pull * scale, 0.0)


STRIP = 32
THIN = 16
LARGE = 1 << 20


class Names:
    def __init__(self, names, refs):
        self.table = dict(zip(names, refs, strict=True))

    def __getattr__(self, name):
        return self.table[name]


SPLIT = (4, 2, 2)
PACK_ROWS = 48
PACK_GRAD_ROWS = 40
POSITION_AT, SMALL_AT, BIAS_AT, LOSS_AT = 0, 64, 96, 97


def merged(block):
    return block.reshape(-1, block.shape[-1])


def start_rows(r, row, at):
    frame = at % LENGTH
    start = r.tokens[pl.ds(pl.multiple_of(row + at, STRIP), STRIP), :].astype(F32)
    return start + r.positions[frame : frame + STRIP, :]


def norm_pass(r):
    count = r.tokens.shape[0]
    rows = 4 * LENGTH

    def body(i, carry):
        row = pl.multiple_of(i * rows, rows)
        for at in range(0, rows, STRIP):
            unit, _ = normalise(start_rows(r, row, at))
            normed = unit * r.small[G1 : G1 + 1, :] + r.small[B1 : B1 + 1, :]
            r.attended[pl.ds(pl.multiple_of(row + at, STRIP), STRIP), :] = normed.astype(BF16)
        r.normed_t[:, pl.ds(row, rows)] = r.attended[pl.ds(row, rows), :].T
        return carry

    lax.fori_loop(0, count // rows, body, 0)


def front(r, pump):
    count, width = r.tokens.shape
    rows = 4 * LENGTH

    def body(i, carry):
        pump(i)
        row = pl.multiple_of(i * rows, rows)
        normed = r.attended[pl.ds(row, rows), :]
        for at in range(0, 3 * width, width):
            r.qkv[pl.ds(row, rows), at : at + width] = dot(
                normed, merged(r.w_qkv[:, :, :, :, at : at + width]), 1, 0
            ).astype(BF16)
        attend_group(r, i)
        return carry

    lax.fori_loop(0, count // rows, body, 0)


def add_grad(ref, index, values):
    ref[index] += values.reshape(ref[index].shape)


def add_columns(ref, values):
    count = ref.shape[-1]
    for k in range(values.shape[1] // count):
        ref[k // 2, k % 2] += values[:, k * count : (k + 1) * count]


def clear(r):
    for ref in (r.g_out, r.g_up, r.g_down):

        def body(z, carry, ref=ref):
            ref[z] = jnp.zeros(ref.shape[1:], F32)
            return carry

        lax.fori_loop(0, ref.shape[0], body, 0)
    for ref in (r.g_actor, r.g_small, r.g_up_bias, r.g_positions, r.head_sums):
        ref[...] = jnp.zeros_like(ref)


def frame_values(r):
    r.causal[...] = causal_bias()
    fresh = DECAY_RATE * r.running[...] + (1.0 - DECAY_RATE) * r.percentiles[...]
    spread = jnp.maximum(1.0, fresh[1:2, :] - fresh[0:1, :])
    seqs = r.game_ids.shape[0]
    game = r.game_ids[...].reshape(seqs, 1)
    slot = lax.broadcasted_iota(jnp.int32, (seqs, spread.shape[1]), 1)
    column = jnp.sum(jnp.where(slot == game, spread, 0.0), 1, keepdims=True)
    count = 8 * LENGTH
    owner = lax.broadcasted_iota(jnp.int32, (8, count), 0)
    frame = lax.broadcasted_iota(jnp.int32, (8, count), 1)
    for k in range(seqs // 8):
        here = slice(k * count, (k + 1) * count)
        near = jnp.where(frame // LENGTH == owner, column[8 * k : 8 * k + 8], 0.0)
        wide = jnp.sum(near, 0, keepdims=True)
        r.advantage[:, here] = (r.returns[here] - r.values[here]).reshape(1, count) / wide
        r.action_row[:, here] = r.actions[here].reshape(1, count)


class Tile:
    def __init__(self, r, side):
        def pick(name):
            return r.table[name, side]

        self.active, self.slope = pick("active"), pick("slope")
        self.two_t, self.unit, self.last = pick("two_t"), pick("unit"), pick("last")
        self.scale = pick("scale")


def middle_part(r, scale):
    count, width = r.tokens.shape
    rows = r.low.shape[0]
    shards = r.w_up.shape[0]
    chunk = r.w_up.shape[-1] // shards
    slots = r.masks.shape[0]
    out_weight = r.w_out
    head_bias = jnp.concatenate(
        [r.actor_bias[...].astype(F32).reshape(slots, 1), jnp.zeros((SLOTS - slots, 1), F32)], 0
    )
    everything = slice(None)
    strips = [slice(at, at + STRIP) for at in range(0, rows, STRIP)]

    def gain(k):
        return r.small[k : k + 1, :]

    def tile_rows(i):
        return pl.ds(pl.multiple_of(i * rows, rows), rows)

    def project(i):
        return dot(r.attended[tile_rows(i), :], merged(out_weight[...]), 1, 0)

    def before(i, t, projected):
        row = pl.multiple_of(i * rows, rows)
        for strip in strips:
            mid = start_rows(r, row, strip.start) + projected[strip]
            unit, spread = normalise(mid)
            r.two_low[strip, :] = (unit * gain(G2) + gain(B2)).astype(BF16)
            t.unit[strip, :] = unit
            t.scale[strip, :] = spread
            t.last[strip, :] = mid + gain(DB)
        t.two_t[...] = r.two_low[...].T

    def columns(j):
        return pl.ds(pl.multiple_of(j * chunk, chunk), chunk)

    def up_weight(j):
        return merged(r.w_up[:, :, :, :, columns(j)])

    def activate(j, t, hidden):
        cols = columns(j)
        bias = r.up_bias[:, cols]
        for at in range(0, rows, THIN):
            value, derivative = gelu_pair(hidden[at : at + THIN] + bias)
            t.active[at : at + THIN, cols] = value.astype(BF16)
            t.slope[at : at + THIN, cols] = derivative.astype(BF16)

    def forward_only(j, t):
        activate(j, t, dot(r.two_low[...], up_weight(j), 1, 0))
        t.last[...] += dot(t.active[:, columns(j)], merged(r.w_down[j]), 1, 0)

    def both_ways(j, here, there):
        cols = columns(j)
        if there is not None:
            hidden = dot(r.two_low[...], up_weight(j), 1, 0)
        hidden_grad = dot(r.low[...], merged(r.w_down[j]), 1, 1)
        add_columns(r.g_down.at[j], dot(r.low_t[...], here.active[:, cols], 1, 0))
        total = r.g_up_bias[:, cols]
        for at in range(0, rows, THIN):
            strip = slice(at, at + THIN)
            part = (hidden_grad[strip] * here.slope[strip, cols].astype(F32)).astype(BF16)
            r.hidden_grad[strip, :] = part
            total += fold_rows(part.astype(F32))
        r.g_up_bias[:, cols] = total
        r.two_in[...] += dot(r.hidden_grad[...], up_weight(j), 1, 1)
        add_grad(
            r.g_up,
            (everything, everything, everything, everything, cols),
            dot(here.two_t[...], r.hidden_grad[...], 1, 0),
        )
        if there is not None:
            activate(j, there, hidden)
            there.last[...] += dot(there.active[:, cols], merged(r.w_down[j]), 1, 0)

    def last_norm(i, t):
        for strip in strips:
            unit, spread = normalise(t.last[strip, :])
            r.low[strip, :] = (unit * gain(GL) + gain(BL)).astype(BF16)
            t.last[strip, :] = unit
            r.scale_last[strip, :] = spread
        return dot(r.actor[...], r.low[...], 1, 1) + head_bias

    def head(i, logits):
        here = tile_rows(i)
        masks = jnp.concatenate(
            [r.masks[:, here], jnp.zeros((SLOTS - slots, rows), jnp.int32)], 0
        )
        loss, pull = policy(logits, masks, r.action_row[:, here], r.advantage[:, here], scale)
        logit_grad = pull.astype(BF16)
        last_in = dot(logit_grad, r.actor[...], 0, 0)
        r.g_actor[...] += dot(logit_grad, r.low[...], 1, 0)
        wide_grad = logit_grad.astype(F32)
        fold = r.head_sums[0:SLOTS, :]
        for at in range(0, rows, 128):
            fold += wide_grad[:, at : at + 128]
        r.head_sums[0:SLOTS, :] = fold
        fold = r.head_sums[SLOTS : SLOTS + 1, :]
        for at in range(0, rows, 128):
            fold += loss[:, at : at + 128]
        r.head_sums[SLOTS : SLOTS + 1, :] = fold
        return last_in

    def last_norm_back(t, last_in):
        sums = [r.g_small[k] for k in (GL, BL, DB)]
        for strip in strips:
            above, unit = last_in[strip], t.last[strip, :]
            grad = norm_back(unit, r.scale_last[strip, :], gain(GL), above)
            sums[0] += fold_rows(above * unit)
            sums[1] += fold_rows(above)
            sums[2] += fold_rows(grad)
            t.last[strip, :] = grad
            r.low[strip, :] = grad.astype(BF16)
        for k, total in zip((GL, BL, DB), sums, strict=True):
            r.g_small[k] = total
        r.low_t[...] = r.low[...].T
        r.two_in[...] = jnp.zeros((rows, width), F32)

    def two_norm_back(i, t):
        row = pl.multiple_of(i * rows, rows)
        sums = [r.g_small[k] for k in (G2, B2)]
        for strip in strips:
            above, unit = r.two_in[strip, :], t.unit[strip, :]
            sums[0] += fold_rows(above * unit)
            sums[1] += fold_rows(above)
            grad = t.last[strip, :] + norm_back(unit, t.scale[strip, :], gain(G2), above)
            r.middle_grad[pl.ds(pl.multiple_of(row + strip.start, STRIP), STRIP), :] = grad
            r.middle_low[strip, :] = grad.astype(BF16)
        for k, total in zip((G2, B2), sums, strict=True):
            r.g_small[k] = total

    def out_back(i):
        here = tile_rows(i)
        add_grad(r.g_out, ..., dot(r.attended[here, :], r.middle_low[...], 0, 0))
        r.attended[here, :] = dot(r.middle_low[...], merged(out_weight[...]), 1, 1).astype(BF16)

    sides = [Tile(r, 0), Tile(r, 1)]
    tiles = count // rows

    def chunks(step):
        def body(j, carry):
            step(j)
            return carry

        lax.fori_loop(0, shards, body, 0)

    def step(i, side, first=False, last=False):
        here, there = sides[side], sides[1 - side]
        projected = None if last else project(i + 1)
        logits = last_norm(i, here)
        if not first:
            two_norm_back(i - 1, there)
        last_in = head(i, logits)
        if not last:
            before(i + 1, there, projected)
        last_norm_back(here, last_in)
        if not first:
            out_back(i - 1)
        chunks(lambda j: both_ways(j, here, None if last else there))

    before(0, sides[0], project(0))
    chunks(lambda j: forward_only(j, sides[0]))
    step(0, 0, first=True)

    def pair(p, carry):
        step(2 * p + 1, 1)
        step(2 * p + 2, 0)
        return carry

    lax.fori_loop(0, (tiles - 2) // 2, pair, 0)
    step(tiles - 1, 1, last=True)
    two_norm_back(tiles - 1, sides[1])
    out_back(tiles - 1)


def attend_back(r, pump):
    count = r.tokens.shape[0]
    rows = 4 * LENGTH

    def body(i, carry):
        pump(i)
        attend_back_group(r, i)
        return carry

    lax.fori_loop(0, count // rows, body, 0)


def qkv_weight_grad(r, third):
    width = r.tokens.shape[1]
    step = width // 2
    for at in range(third * width, (third + 1) * width, step):
        values = dot(r.normed_t[...], r.qkv[:, at : at + step], 1, 0)
        r.g_qkv[:, :, :, :, at : at + step] = values.reshape(r.g_qkv.shape[:4] + (step,))


def start_back(r, pump, tile_done):
    count = r.tokens.shape[0]
    rows = 4 * LENGTH
    gain = r.small[G1 : G1 + 1, :]

    def body(i, carry):
        pump(i)
        row = pl.multiple_of(i * rows, rows)
        one_in = dot(r.qkv[pl.ds(row, rows), :], merged(r.w_qkv[...]), 1, 1)
        sums = [r.g_small[k] for k in (G1, B1)]
        for at in range(0, rows, STRIP):
            there = pl.ds(pl.multiple_of(row + at, STRIP), STRIP)
            unit, scale = normalise(start_rows(r, row, at))
            above = one_in[at : at + STRIP]
            sums[0] += fold_rows(above * unit)
            sums[1] += fold_rows(above)
            grad = r.middle_grad[there, :] + norm_back(unit, scale, gain, above)
            r.middle_grad[there, :] = grad
            frame = at % LENGTH
            r.g_positions[frame : frame + STRIP, :] += grad
        for k, total in zip((G1, B1), sums, strict=True):
            r.g_small[k] = total
        tile_done(i)
        return carry

    lax.fori_loop(0, count // rows, body, 0)


def pack_shards(r):
    part = r.positions_in.shape[0]
    slots = r.masks.shape[0]
    rows = [
        ref[...].astype(F32).reshape(1, part)
        for ref in (r.gain1, r.bias1, r.gain2, r.bias2, r.bias_down, r.gain3, r.bias3)
    ]
    rows += [r.actor_in[...].astype(F32), jnp.zeros((32 - 7 - slots, part), F32)]
    features = jnp.concatenate(
        [r.positions_in[...].astype(F32), jnp.concatenate(rows, 0).T, jnp.zeros((part, 32), F32)], 1
    )
    bias = r.up_bias_in[...].astype(F32).reshape(1, 128)
    packed = jnp.concatenate([features, bias, jnp.zeros((PACK_ROWS - part - 1, 128), F32)], 0)
    r.pack_own[...] = packed.astype(BF16)


def unpack_shards(r):
    slots = r.masks.shape[0]
    blocks = r.pack[...].astype(F32).reshape(-1, PACK_ROWS, 128)
    part = r.positions_in.shape[0]
    features = merged(blocks[:, :part, :]).T
    r.positions[...] = features[POSITION_AT : POSITION_AT + LENGTH]
    small = features[SMALL_AT : SMALL_AT + 32]
    r.small[...] = small[0:8]
    width = small.shape[1]
    r.actor[...] = jnp.concatenate(
        [small[7 : 7 + slots], jnp.zeros((SLOTS - slots, width), F32)], 0
    ).astype(BF16)
    r.up_bias[...] = jnp.concatenate(
        [blocks[f, part : part + 1, :] for f in range(blocks.shape[0])], 1
    )


def small_rows(r):
    slots = r.masks.shape[0]
    rows = [jnp.sum(r.g_small[k], 0, keepdims=True) for k in range(7)]
    return jnp.concatenate(
        rows + [r.g_actor[0:slots, :], jnp.zeros((32 - 7 - slots, rows[0].shape[1]), F32)], 0
    )


def pack_grads(r):
    width = r.tokens.shape[1]
    part = r.positions_in.shape[0]
    features = jnp.concatenate(
        [r.g_positions[...], small_rows(r), jnp.zeros((128 - SMALL_AT - 32, width), F32)], 0
    ).T
    sums = jnp.sum(r.head_sums[0 : SLOTS + 8, :], 1, keepdims=True)
    lane = lax.broadcasted_iota(jnp.int32, (part, 128), 1)
    bias = jnp.sum(r.g_up_bias[...], 0, keepdims=True)
    shape = r.g_pack.shape
    for f in range(width // part):
        block = features[f * part : (f + 1) * part]
        block = jnp.where(lane == BIAS_AT, sums[0:SLOTS], block)
        block = jnp.where(lane == LOSS_AT, sums[SLOTS : SLOTS + 1], block)
        owner = (f // 4, f // 2 % 2, f % 2)
        rows = [block, bias[:, f * 128 : (f + 1) * 128], jnp.zeros((shape[3] - part - 1, 128), F32)]
        r.g_pack[owner] = jnp.concatenate(rows, 0)


GATHERS = 9
REDUCES = (
    (128, 512, BF16),
    (2048, 32, BF16),
    (512, 32, BF16),
    (512, 32, BF16),
    (512, 32, BF16),
    (512, 32, BF16),
    (128, PACK_GRAD_ROWS, F32),
)


class Place:
    def __init__(self):
        self.x = lax.axis_index("dp")
        f = lax.axis_index("fsdp")
        self.z, self.y, self.c = f // 4, f // 2 % 2, f % 2

    def at(self, x=None, z=None, y=None, c=None):
        pick = lambda new, old: old if new is None else new
        f = pick(z, self.z) * 4 + pick(y, self.y) * 2 + pick(c, self.c)
        return (pick(x, self.x), f)

    def z_partner(self, k):
        return (self.z + 1 - 2 * (self.z % 2), (self.z + 2) % 4, 3 - self.z)[k]

    def partners(self):
        return [self.at(z=self.z_partner(k)) for k in range(3)] + [
            self.at(y=1 - self.y),
            self.at(c=1 - self.c),
            self.at(x=1 - self.x),
        ]


class Gather:
    def __init__(self, r, place, index, full, own, at, count):
        cols = slice(at, at + count)
        self.full, self.own, self.cols, self.place = full, own, cols, place
        p = place

        def copy(src, dst, k, device):
            return pltpu.make_async_remote_copy(
                src_ref=src,
                dst_ref=dst,
                send_sem=r.gather_send.at[index, k],
                recv_sem=r.gather_recv.at[index, k],
                device_id=device,
                device_id_type=MESH,
            )

        mine = full.at[p.z, p.y, p.c, :, cols]
        self.z = [copy(own.at[:, cols], mine, k, p.at(z=p.z_partner(k))) for k in range(3)]
        line = full.at[:, p.y, p.c, :, cols]
        self.y = copy(line, line, 3, p.at(y=1 - p.y))
        plane = full.at[:, :, p.c, :, cols]
        self.c = copy(plane, plane, 4, p.at(c=1 - p.c))

    def start_z(self):
        for copy in self.z:
            copy.start()
        p = self.place
        self.full[p.z, p.y, p.c, :, self.cols] = self.own[:, self.cols]

    def start_y(self):
        for copy in self.z:
            copy.wait_recv()
        self.y.start()

    def start_c(self):
        self.y.wait_recv()
        self.c.start()

    def ready(self):
        self.c.wait_recv()

    def close(self):
        for copy in self.z + [self.y, self.c]:
            copy.wait_send()


class Reduce:
    def __init__(self, r, place, index, grad, at=0):
        count, _, kind = REDUCES[index]
        self.grad, self.cols, self.place, self.kind = grad, slice(at, at + count), place, kind
        p = place
        self.buffers = [r.table[index, part] for part in range(len(REDUCE_LEADS))]
        sc, rc, ry, rz, rx = self.buffers
        self.sy, self.sz, self.sx = sc.at[:, 0], [sc.at[k, 1] for k in range(3)], sc.at[3, 1]

        def copy(src, dst, k, device):
            return pltpu.make_async_remote_copy(
                src_ref=src,
                dst_ref=dst,
                send_sem=r.reduce_send.at[index, k],
                recv_sem=r.reduce_recv.at[index, k],
                device_id=device,
                device_id_type=MESH,
            )

        self.c = copy(sc, rc, 0, p.at(c=1 - p.c))
        self.y = copy(self.sy, ry, 1, p.at(y=1 - p.y))
        self.z = [copy(self.sz[k], rz.at[k], 2 + k, p.at(z=p.z_partner(k))) for k in range(3)]
        self.x = copy(self.sx, rx, 5, p.at(x=1 - p.x))

    def start_c(self):
        sc, p = self.buffers[0], self.place

        def body(z, carry):
            sc[z] = self.grad[z, :, 1 - p.c, :, self.cols].astype(self.kind)
            return carry

        lax.fori_loop(0, 4, body, 0)
        self.c.start()

    def start_y(self):
        rc, sy = self.buffers[1], self.sy
        p = self.place
        self.c.wait()

        def body(z, carry):
            away = self.grad[z, 1 - p.y, p.c, :, self.cols] + rc[z, 1 - p.y].astype(F32)
            sy[z] = away.astype(self.kind)
            self.grad[z, p.y, p.c, :, self.cols] += rc[z, p.y].astype(F32)
            return carry

        lax.fori_loop(0, 4, body, 0)
        self.y.start()

    def start_z(self):
        ry, sz = self.buffers[2], self.sz
        p = self.place
        self.y.wait_recv()
        for k in (2, 1, 0):
            owner = p.z_partner(k)
            away = self.grad[owner, p.y, p.c, :, self.cols] + ry[owner].astype(F32)
            sz[k][...] = away.astype(self.kind)
            self.z[k].start()
        self.grad[p.z, p.y, p.c, :, self.cols] += ry[p.z].astype(F32)

    def start_x(self):
        rz, sx = self.buffers[3], self.sx
        p = self.place
        for copy in self.z:
            copy.wait_recv()
        near = self.grad[p.z, p.y, p.c, :, self.cols] + rz[0].astype(F32)
        sx[...] = (near + (rz[1].astype(F32) + rz[2].astype(F32))).astype(self.kind)
        self.x.start()

    def finish(self, out):
        sx, rx = self.sx, self.buffers[4]
        self.x.wait_recv()
        out[:, self.cols] = sx[...].astype(F32) + rx[...].astype(F32)

    def close(self):
        for copy in self.z + [self.y, self.x]:
            copy.wait_send()


REDUCE_LEADS = ((4, 2), (4, 2), (4,), (3,), ())


def layer_scratch(row_count, width, hidden_width, shards):
    tile = 256
    seqs = row_count // LENGTH
    pairs = dict(
        active=((tile, hidden_width), BF16),
        slope=((tile, hidden_width), BF16),
        two_t=((width, tile), BF16),
        unit=((tile, width), F32),
        last=((tile, width), F32),
        scale=((tile, 1), F32),
    )
    both = {(name, side): item for name, item in pairs.items() for side in range(2)}
    return both | dict(
        tokens=((row_count, width), BF16),
        middle_grad=((row_count, width), F32),
        normed_t=((width, row_count), BF16),
        qkv=((row_count, 3 * width), BF16),
        attended=((row_count, width), BF16),
        totals=((seqs, width), F32),
        causal=((LENGTH, WIDE), F32),
        advantage=((1, row_count), F32),
        action_row=((1, row_count), jnp.int32),
        two_low=((tile, width), BF16),
        low=((tile, width), BF16),
        low_t=((width, tile), BF16),
        middle_low=((tile, width), BF16),
        hidden_grad=((tile, hidden_width // 4), BF16),
        two_in=((tile, width), F32),
        scale_last=((tile, 1), F32),
        local_sem=pltpu.SemaphoreType.DMA((2,)),
    )


def grad_shapes(width, hidden_width, shards):
    split = SPLIT
    part, hidden_part = width // shards, hidden_width // shards
    return dict(
        g_qkv=(split + (part, 3 * width), F32),
        g_out=(split + (part, width), F32),
        g_up=(split + (part, hidden_width), F32),
        g_down=(split + (width, hidden_part), F32),
        g_actor=((SLOTS, width), F32),
        g_small=((7, 8, width), F32),
        g_up_bias=((8, hidden_width), F32),
        g_positions=((LENGTH, width), F32),
        head_sums=((SLOTS + 8, 128), F32),
    )


def at_step(i, table):
    for step, actions in table.items():

        @pl.when(i == step)
        def _(actions=actions):
            for action in actions:
                action()


def spread_kernel(names, scale, *refs):
    r = Names(names, refs)
    place = Place()
    load = pltpu.make_async_copy(r.tokens_in, r.tokens, r.local_sem.at[0])
    load.start()
    partners = place.partners()
    barrier = pltpu.get_barrier_semaphore()
    for device in partners:
        pl.semaphore_signal(barrier, inc=1, device_id=device, device_id_type=MESH)
    pack_shards(r)
    pl.semaphore_wait(barrier, len(partners))
    width, hidden_width = r.w_out.shape[-1], r.w_up.shape[-1]
    plan = [(r.pack, r.pack_own, 0, 128)]
    plan += [(r.w_qkv, r.qkv_in, k * width, width) for k in range(3)]
    plan += [(r.w_out, r.out_in, 0, width)]
    plan += [(r.w_up, r.up_in, k * hidden_width // 2, hidden_width // 2) for k in range(2)]
    plan += [(r.w_down, r.down_in, k * width // 2, width // 2) for k in range(2)]
    gathers = [Gather(r, place, k, *item) for k, item in enumerate(plan)]
    pack, q, k, v, out, up0, up1, down0, down1 = gathers
    pack.start_z()
    q.start_z()
    k.start_z()
    v.start_z()
    pack.start_y()
    q.start_y()
    pack.start_c()
    clear(r)
    frame_values(r)
    pack.ready()
    unpack_shards(r)
    k.start_y()
    q.start_c()
    load.wait()
    out.start_z()
    up0.start_z()
    norm_pass(r)
    v.start_y()
    k.start_c()
    up1.start_z()
    down0.start_z()
    down1.start_z()
    v.start_c()
    for group in (q, k, v):
        group.ready()

    front(
        r,
        lambda i: at_step(
            i,
            {
                1: [out.start_y],
                2: [out.start_c],
                3: [up0.start_y],
                5: [up1.start_y, up0.start_c],
                7: [down0.start_y, up1.start_c],
                9: [down1.start_y, down0.start_c],
            },
        ),
    )
    down1.start_c()
    for group in (out, up0, up1, down0, down1):
        group.ready()
    middle_part(r, scale)

    plan = [(r.g_down,), (r.g_up,), (r.g_out,)]
    plan += [(r.g_qkv, k * width) for k in range(3)] + [(r.g_pack,)]
    reduces = [Reduce(r, place, k, *item) for k, item in enumerate(plan)]
    down, up, out, q, k, v, pack = reduces
    down.start_c()
    up.start_c()
    out.start_c()
    attend_back(
        r,
        lambda i: at_step(
            i,
            {
                1: [down.start_y],
                2: [up.start_y],
                3: [out.start_y],
                5: [down.start_z],
                8: [up.start_z, down.start_x],
                9: [out.start_z],
            },
        ),
    )
    for third, group in enumerate((q, k, v)):
        qkv_weight_grad(r, third)
        group.start_c()
        if third:
            (q, k)[third - 1].start_y()
    v.start_y()
    up.start_x()
    out.start_x()

    def stored(i):
        rows = pl.ds(pl.multiple_of(i * 4 * LENGTH, 4 * LENGTH), 4 * LENGTH)
        return pltpu.make_async_copy(
            r.middle_grad.at[rows, :], r.tokens_grad.at[rows, :], r.store_sem.at[i]
        )

    start_back(
        r,
        lambda i: at_step(
            i, {2: [q.start_z], 4: [k.start_z], 6: [v.start_z, q.start_x], 8: [k.start_x]}
        ),
        lambda i: stored(i).start(),
    )
    pack_grads(r)
    pack.start_c()
    v.start_x()
    pack.start_y()
    down.finish(r.down_out)
    up.finish(r.up_out)
    out.finish(r.out_out)
    pack.start_z()
    for group in (q, k, v):
        group.finish(r.qkv_out)
    pack.start_x()
    for i in range(r.middle_grad.shape[0] // (4 * LENGTH)):
        stored(i).wait()
    for group in gathers + reduces:
        group.close()
    pack.finish(r.pack_out)


def finish_kernel(names, count, *refs):
    r = Names(names, refs)
    step = 4 * LENGTH
    parts = [pl.ds(at, step) for at in range(0, r.tokens.shape[0], step)]
    loads = [
        pltpu.make_async_copy(r.tokens.at[part, :], r.held.at[part, :], r.load_sem.at[k])
        for k, part in enumerate(parts)
    ]
    stores = [
        pltpu.make_async_copy(r.held.at[part, :], r.o_tokens.at[part, :], r.store_sem.at[k])
        for k, part in enumerate(parts)
    ]
    for load in loads:
        load.start()
    r.o_qkv[...] = r.qkv[...]
    r.o_out[...] = r.out[...]
    r.o_up[...] = r.up[...]
    r.o_down[...] = r.down[...].T
    r.o_stats[...] = DECAY_RATE * r.running[...] + (1.0 - DECAY_RATE) * r.percentiles[...]
    part, positions = r.o_positions.shape
    slots = r.o_actor.shape[0]
    features = r.pack[0:part, :]
    r.o_positions[...] = features[:, POSITION_AT : POSITION_AT + positions]
    turned = features.T
    vectors = (r.gain1, r.bias1, r.gain2, r.bias2, r.bias_down, r.gain3, r.bias3)
    for k, ref in enumerate(vectors):
        ref[...] = turned[SMALL_AT + k : SMALL_AT + k + 1, :].reshape(part)
    r.o_actor[...] = turned[SMALL_AT + 7 : SMALL_AT + 7 + slots, :]
    r.o_actor_bias[...] = turned[BIAS_AT : BIAS_AT + 1, :].reshape(part)[0:slots]
    r.o_loss[...] = features[0:1, LOSS_AT : LOSS_AT + 1] * (1.0 / count)
    r.o_up_bias[...] = r.pack[part : part + 1, :].reshape(128)
    for load, store in zip(loads, stores, strict=True):
        load.wait()
        store.start()
    for store in stores:
        store.wait()


def local_kernel(names, scale, *refs):
    r = Names(names, refs)
    load = pltpu.make_async_copy(r.tokens_in, r.tokens, r.local_sem.at[0])
    load.start()
    clear(r)
    frame_values(r)
    load.wait()
    norm_pass(r)
    front(r, lambda i: None)
    middle_part(r, scale)
    attend_back(r, lambda i: None)
    for third in range(3):
        qkv_weight_grad(r, third)
    start_back(r, lambda i: None, lambda i: None)
    store = pltpu.make_async_copy(r.middle_grad, r.tokens_grad, r.local_sem.at[1])
    store.start()
    store.wait()


def run(kernel, constant, ins, outs, scratch, flops=0, side_effects=False, collective=None):
    vmem = pl.BlockSpec(memory_space=pltpu.VMEM)
    anywhere = pl.BlockSpec(memory_space=pl.ANY)
    in_specs = [anywhere if array.size > LARGE else vmem for array in ins.values()]
    out_specs = [anywhere if math.prod(shape) > LARGE else vmem for shape, _ in outs.values()]
    return pl.pallas_call(
        functools.partial(kernel, (*ins, *outs, *scratch), constant),
        out_shape=[jax.ShapeDtypeStruct(shape, kind) for shape, kind in outs.values()],
        in_specs=in_specs,
        out_specs=out_specs,
        scratch_shapes=[
            item if not isinstance(item, tuple) else pltpu.VMEM(item[0], item[1])
            for item in scratch.values()
        ],
        compiler_params=pltpu.CompilerParams(
            vmem_limit_bytes=VMEM_BYTES, has_side_effects=side_effects, collective_id=collective
        ),
        cost_estimate=pl.CostEstimate(flops=flops, bytes_accessed=1 << 24, transcendentals=0),
    )(*ins.values())


def on_device(
    tokens,
    positions,
    norm_one_gain,
    norm_one_bias,
    qkv_weight,
    out_weight,
    norm_two_gain,
    norm_two_bias,
    up_weight,
    up_bias,
    down_weight,
    down_bias,
    final_gain,
    final_bias,
    actor_weight,
    actor_bias,
    actions,
    action_masks,
    game_ids,
    returns,
    values,
    running,
    percentiles,
):
    row_count, width = tokens.shape
    seq_count = row_count // LENGTH
    hidden_width = up_weight.shape[1]
    slots = actor_weight.shape[1]
    fsdp = lax.axis_size("fsdp")
    device_count = lax.axis_size("dp") * fsdp
    token_total = row_count * device_count
    scale = float(seq_count * device_count) / token_total
    flops = 6 * row_count * width * (4 * width + 2 * hidden_width)
    part, hidden_part = width // fsdp, hidden_width // fsdp

    vectors = dict(
        gain1=norm_one_gain,
        bias1=norm_one_bias,
        gain2=norm_two_gain,
        bias2=norm_two_bias,
        bias_down=down_bias,
        gain3=final_gain,
        bias3=final_bias,
    )
    stats = dict(running=running, percentiles=percentiles)
    frames = stats | dict(
        tokens_in=tokens,
        actor_bias=actor_bias,
        actions=actions,
        masks=action_masks.T,
        game_ids=game_ids,
        returns=returns,
        values=values,
    )
    scratch = layer_scratch(row_count, width, hidden_width, 16)
    grads = grad_shapes(width, hidden_width, 16)
    weight_shapes = dict(
        w_qkv=(SPLIT + (width // 16, 3 * width), BF16),
        w_out=(SPLIT + (width // 16, width), BF16),
        w_up=(SPLIT + (width // 16, hidden_width), BF16),
        w_down=(SPLIT + (hidden_width // 16, width), BF16),
    )

    if fsdp == 16 and lax.axis_size("dp") == 2:
        ins = frames | vectors
        ins |= dict(qkv_in=qkv_weight, out_in=out_weight, up_in=up_weight, down_in=down_weight)
        ins |= dict(up_bias_in=up_bias, positions_in=positions.T, actor_in=actor_weight.T)
        shard_grads = dict(
            qkv_out=((part, 3 * width), F32),
            out_out=((part, width), F32),
            up_out=((part, hidden_width), F32),
            down_out=((width, hidden_part), F32),
        )
        outs = dict(
            tokens_grad=((row_count, width), F32), pack_out=((PACK_GRAD_ROWS, 128), F32)
        )
        scratch |= grads | weight_shapes
        scratch |= dict(
            pack=(SPLIT + (PACK_ROWS, 128), BF16),
            pack_own=((PACK_ROWS, 128), BF16),
            g_pack=(SPLIT + (PACK_GRAD_ROWS, 128), F32),
            positions=((LENGTH, width), F32),
            small=((8, width), F32),
            actor=((SLOTS, width), BF16),
            up_bias=((1, hidden_width), F32),
            gather_send=pltpu.SemaphoreType.DMA((GATHERS, 5)),
            gather_recv=pltpu.SemaphoreType.DMA((GATHERS, 5)),
            reduce_send=pltpu.SemaphoreType.DMA((len(REDUCES), 6)),
            reduce_recv=pltpu.SemaphoreType.DMA((len(REDUCES), 6)),
            store_sem=pltpu.SemaphoreType.DMA((row_count // (4 * LENGTH),)),
        )
        for index, (count, rows, kind) in enumerate(REDUCES):
            for item, lead in enumerate(REDUCE_LEADS):
                scratch[index, item] = (lead + (rows, count), kind)
        tokens_grad, pack, qkv_g, out_g, up_g, down_g = run(
            spread_kernel, scale, ins, outs | shard_grads, scratch, flops, True, 0
        )
        vector = ((part,), F32)
        final = dict(
            o_loss=((1, 1), F32),
            o_stats=(running.shape, F32),
            o_positions=((part, LENGTH), F32),
            o_qkv=shard_grads["qkv_out"],
            o_out=shard_grads["out_out"],
            o_up=shard_grads["up_out"],
            o_down=((hidden_part, width), F32),
            o_up_bias=((hidden_part,), F32),
            o_actor=((slots, part), F32),
            o_actor_bias=((slots,), F32),
            o_tokens=((row_count, width), F32),
        )
        copies = pltpu.SemaphoreType.DMA((row_count // (4 * LENGTH),))
        done = run(
            finish_kernel,
            token_total,
            stats
            | dict(pack=pack, qkv=qkv_g, out=out_g, up=up_g, down=down_g, tokens=tokens_grad),
            final | dict.fromkeys(vectors, vector),
            dict(held=((row_count, width), F32), load_sem=copies, store_sem=copies),
        )
        loss, new_stats, pos_g, qkv_g, out_g, up_g, down_g = done[:7]
        up_bias_g, actor_g, actor_bias_g, tokens_grad = done[7:11]
        gain1, bias1, gain2, bias2, bias_down, gain3, bias3 = done[11:]
        return (
            loss.reshape(()),
            new_stats,
            tokens_grad,
            pos_g.T,
            gain1,
            bias1,
            qkv_g,
            out_g,
            gain2,
            bias2,
            up_g,
            up_bias_g,
            down_g,
            bias_down,
            gain3,
            bias3,
            actor_g.T,
            actor_bias_g,
        )

    def gather(array, axis):
        return lax.all_gather(array, "fsdp", axis=axis, tiled=True)

    packed = gather(
        jnp.concatenate([jnp.stack(list(vectors.values())), actor_weight.T, positions], 0), 1
    )
    fulls = [gather(weight, 0) for weight in (qkv_weight, out_weight, up_weight, down_weight)]
    ins = frames | {
        name: full.reshape(weight_shapes[name][0])
        for name, full in zip(weight_shapes, fulls, strict=True)
    }
    ins |= dict(
        positions=packed[7 + slots :].astype(F32),
        small=jnp.pad(packed[0:7].astype(F32), ((0, 1), (0, 0))),
        actor=jnp.pad(packed[7 : 7 + slots], ((0, SLOTS - slots), (0, 0))),
        up_bias=gather(up_bias, 0).astype(F32).reshape(1, hidden_width),
    )
    outs = dict(tokens_grad=((row_count, width), F32)) | grads
    tokens_grad, *sums = run(local_kernel, scale, ins, outs, scratch, flops)
    sums = Names(grads, sums)

    def scatter(array, axis):
        piece = lax.psum_scatter(array, "fsdp", scatter_dimension=axis, tiled=True)
        return lax.psum(piece.astype(BF16), "dp").astype(F32)

    down_sum = jnp.swapaxes(sums.g_down, 3, 4)
    qkv_part, out_part, up_part, down_part = (
        scatter(merged(grad), 0) for grad in (sums.g_qkv, sums.g_out, sums.g_up, down_sum)
    )
    rows = [jnp.sum(sums.g_small, 1), sums.g_actor[:slots], sums.g_positions]
    side = scatter(jnp.concatenate(rows, 0), 1)
    up_bias_part = scatter(jnp.sum(sums.g_up_bias, 0), 0)
    head_total = lax.psum(jnp.sum(sums.head_sums[: SLOTS + 1], 1), ("dp", "fsdp"))
    return (
        head_total[SLOTS] / token_total,
        DECAY_RATE * running + (1.0 - DECAY_RATE) * percentiles,
        tokens_grad,
        side[7 + slots :],
        side[G1],
        side[B1],
        qkv_part,
        out_part,
        side[G2],
        side[B2],
        up_part,
        up_bias_part,
        down_part,
        side[DB],
        side[GL],
        side[BL],
        side[7 : 7 + slots].T,
        head_total[:slots],
    )


def solution(mesh):
    rows, cols, both = P(("dp", "fsdp"), None), P(None, "fsdp"), P(("dp", "fsdp"))
    weight, vector, whole = P("fsdp", None), P("fsdp"), P()
    in_specs = (rows, cols, vector, vector, weight, weight, vector, vector, weight, vector)
    in_specs += (weight, vector, vector, vector, weight, whole, both, rows, both, both, both)
    in_specs += (whole, whole)
    out_specs = (whole, whole, rows, cols, vector, vector, weight, weight, vector, vector)
    out_specs += (weight, vector, weight, vector, vector, vector, weight, whole)
    return jax.shard_map(
        on_device, mesh=mesh, in_specs=in_specs, out_specs=out_specs, check_vma=False
    )
```

time: 907 us -> 218 us (0.24); the launches traced: 897 us -> 218 us
  matrix products: 239 us -> 0 us
  waiting for transfers between devices: 233 us -> 0 us
  blocking collectives: 220 us -> 0 us
  Pallas kernels: 0 us -> 217 us
  local copies, waits for them, and re-layouts: 112 us -> 0 us
  other arithmetic: 72.6 us -> 0 us
  between operations: 19.3 us -> 0.83 us
    dot_general x49 -> x0, matrix products: 238 us -> none  [the longest x1 55.2 us: on_device(): jnp.dot(two_low, up_full, preferred_element_type=jnp.float32)]
    pallas_call x0 -> x2, Pallas kernels: none -> 217 us  [run(): pl.pallas_call(functools.partial(kernel, (*ins, *outs, *scratch), constan...]
    reduce_scatter x4 -> x0, waiting for transfers between devices: 207 us -> none  [the longest x1 74.3 us: on_device(): lax.psum_scatter(down_grad, 'fsdp', scatter_dimension=0, tiled=True)]
    unnamed x2 -> x0, blocking collectives: 95 us -> none
    all_gather x4 -> x0, blocking collectives: 75.9 us -> none  [the longest x1 21.6 us: on_device(): lax.all_gather(out_weight, 'fsdp', axis=0, tiled=True)]
    psum x2 -> x0, blocking collectives: 49.1 us -> none  [the longest x1 39.9 us: on_device(): lax.psum((local_loss, actor_bias_grad), ('dp', 'fsdp'))]
    reshape x4 -> x0, local copies, waits for them, and re-layouts: 38.2 us -> none  [the longest x1 14.2 us: on_device(): mixed_rows.reshape(block_count, block_groups, GROUP, 3, HEADS, HEAD)]
    reduce_sum x19 -> x0, other arithmetic: 25.6 us -> none  [the longest x3 10.7 us: layer_norm(): centred = values - jnp.mean(values, -1, keepdims=True)]
  transfers between devices with their start and end apart: 10 -> 0, of which waited for: 5 -> 0; matrix products, arithmetic and copies ran while one was open for 26% -> 0% of each run, Pallas kernels for 0% -> 0%
where the time goes in v1:
time: 218 us
  Pallas kernels  217 us (100%)
    pallas_call x2, Pallas kernels, run(): pl.pallas_call(functools.partial(kernel, (*ins, *outs, *scratch), constan...  217 us

profile of v1, /device:TPU:0, one launch (start us, length us, event | category | flops | bytes accessed | tf_op | source)
XLA Modules:
  0.0 217.6 jit_solution(6363833473081636148)
XLA Ops:
  0.7 209.9 %shard_map.358 = (f32[2560,512]{1,0:T(8,128)}, f32[40,128]{1,0:T(8,128)}, f32[32,1536]{1,0:T(8,128)}, f32[32,512]{1,0:T(8,128)}, f32[32,2048]{1,0:T(8,128)}, /*index=5*/f32[512,128]{1,0:T(8,128)}) custom-call(f32[2,26]{1,0:T(2,128)} %refs_0_.3, f32[2,26]{1,0:T(2,128)} %refs_1_.3, bf16[2560,512]{1,0:T(8,128)(2,1)} %refs_2_.1, bf16[18]{0:T(256)(128)(2,1)} %refs_3_.1, ...), custom_call_target="tpu_custom_call" | custom-call | flops 48318382080 | bytes 16777216 | tf_op jit(solution)/shard_map/pallas_call | solution.py:1003
  210.6 6.9 %shard_map.359 = (f32[1,1]{1,0:T(1,128)}, f32[2,26]{1,0:T(2,128)}, f32[32,64]{1,0:T(8,128)}, f32[32,1536]{1,0:T(8,128)}, f32[32,512]{1,0:T(8,128)}, /*index=5*/f...) custom-call(f32[2,26]{1,0:T(2,128)} %refs_0_.3, ...), custom_call_target="tpu_custom_call" | custom-call | bytes 16777216 | tf_op jit(solution)/shard_map/pallas_call | solution.py:1003

commit v2 on v1

--- a/solution.py
+++ b/solution.py
@@ -312,7 +312,7 @@
         self.scale = pick("scale")
 
 
-def middle_part(r, scale):
+def middle_part(r, scale, arrive):
     count, width = r.tokens.shape
     rows = r.low.shape[0]
     shards = r.w_up.shape[0]
@@ -472,6 +472,7 @@
         chunks(lambda j: both_ways(j, here, None if last else there))
 
     before(0, sides[0], project(0))
+    arrive()
     chunks(lambda j: forward_only(j, sides[0]))
     step(0, 0, first=True)
 
@@ -596,13 +597,13 @@
 
 GATHERS = 9
 REDUCES = (
-    (128, 512, BF16),
-    (2048, 32, BF16),
-    (512, 32, BF16),
-    (512, 32, BF16),
-    (512, 32, BF16),
-    (512, 32, BF16),
-    (128, PACK_GRAD_ROWS, F32),
+    (128, 512, BF16, False),
+    (2048, 32, BF16, True),
+    (512, 32, BF16, True),
+    (512, 32, BF16, False),
+    (512, 32, BF16, False),
+    (512, 32, BF16, True),
+    (128, PACK_GRAD_ROWS, F32, False),
 )
 
 
@@ -628,76 +629,95 @@
         ]
 
 
+def remote(r_send, r_recv, index):
+    def copy(src, dst, k, device):
+        return pltpu.make_async_remote_copy(
+            src_ref=src,
+            dst_ref=dst,
+            send_sem=r_send.at[index, k],
+            recv_sem=r_recv.at[index, k],
+            device_id=device,
+            device_id_type=MESH,
+        )
+
+    return copy
+
+
 class Gather:
-    def __init__(self, r, place, index, full, own, at, count):
-        cols = slice(at, at + count)
-        self.full, self.own, self.cols, self.place = full, own, cols, place
+    def __init__(self, r, place, index, full, own, at, count, halved=False):
         p = place
-
-        def copy(src, dst, k, device):
-            return pltpu.make_async_remote_copy(
-                src_ref=src,
-                dst_ref=dst,
-                send_sem=r.gather_send.at[index, k],
-                recv_sem=r.gather_recv.at[index, k],
-                device_id=device,
-                device_id_type=MESH,
-            )
-
-        mine = full.at[p.z, p.y, p.c, :, cols]
-        self.z = [copy(own.at[:, cols], mine, k, p.at(z=p.z_partner(k))) for k in range(3)]
-        line = full.at[:, p.y, p.c, :, cols]
+        copy = remote(r.gather_send, r.gather_recv, index)
+        cols = part = slice(at, at + count)
+        if halved:
+            part = pl.ds(pl.multiple_of(at + p.x * (count // 2), 128), count // 2)
+        self.full, self.own, self.part, self.place = full, own, part, place
+        mine = full.at[p.z, p.y, p.c, :, part]
+        self.z = [copy(own.at[:, part], mine, k, p.at(z=p.z_partner(k))) for k in range(3)]
+        line = full.at[:, p.y, p.c, :, part]
         self.y = copy(line, line, 3, p.at(y=1 - p.y))
+        plane = full.at[:, :, p.c, :, part]
+        self.x = copy(plane, plane, 4, p.at(x=1 - p.x)) if halved else None
         plane = full.at[:, :, p.c, :, cols]
-        self.c = copy(plane, plane, 4, p.at(c=1 - p.c))
+        self.c = copy(plane, plane, 5, p.at(c=1 - p.c))
 
     def start_z(self):
         for copy in self.z:
             copy.start()
         p = self.place
-        self.full[p.z, p.y, p.c, :, self.cols] = self.own[:, self.cols]
+        self.full[p.z, p.y, p.c, :, self.part] = self.own[:, self.part]
 
     def start_y(self):
         for copy in self.z:
             copy.wait_recv()
         self.y.start()
 
+    def start_x(self):
+        self.y.wait_recv()
+        self.x.start()
+
     def start_c(self):
-        self.y.wait_recv()
+        (self.y if self.x is None else self.x).wait_recv()
         self.c.start()
 
     def ready(self):
         self.c.wait_recv()
 
     def close(self):
-        for copy in self.z + [self.y, self.c]:
+        for copy in self.z + [self.y, self.c] + ([] if self.x is None else [self.x]):
             copy.wait_send()
 
 
 class Reduce:
     def __init__(self, r, place, index, grad, at=0):
-        count, _, kind = REDUCES[index]
-        self.grad, self.cols, self.place, self.kind = grad, slice(at, at + count), place, kind
+        count, _, kind, halved = REDUCES[index]
+        self.grad, self.place, self.kind, self.halved = grad, place, kind, halved
         p = place
-        self.buffers = [r.table[index, part] for part in range(len(REDUCE_LEADS))]
-        sc, rc, ry, rz, rx = self.buffers
-        self.sy, self.sz, self.sx = sc.at[:, 0], [sc.at[k, 1] for k in range(3)], sc.at[3, 1]
-
-        def copy(src, dst, k, device):
-            return pltpu.make_async_remote_copy(
-                src_ref=src,
-                dst_ref=dst,
-                send_sem=r.reduce_send.at[index, k],
-                recv_sem=r.reduce_recv.at[index, k],
-                device_id=device,
-                device_id_type=MESH,
-            )
-
+        copy = remote(r.reduce_send, r.reduce_recv, index)
+        self.cols = slice(at, at + count)
+        self.buffers = [r.table[index, part] for part in range(len(reduce_leads(halved)))]
+        sc, rc, ry, rz, rx = self.buffers[:5]
+        keep = count
+        self.part = self.cols
+        if halved:
+            keep = count // 2
+            self.part = self.half(at, keep, p.x)
+            self.away = self.half(at, keep, 1 - p.x)
+            self.local, self.local_away = self.half(0, keep, p.x), self.half(0, keep, 1 - p.x)
+            self.sx1 = sc.at[:, :, :, 0:keep]
+            self.x1 = copy(self.sx1, self.buffers[5], 6, p.at(x=1 - p.x))
+        tail = slice(count - keep, count)
+        self.sy = sc.at[:, 0, :, tail]
+        self.sz = [sc.at[k, 1, :, tail] for k in range(3)]
+        self.sx = sc.at[3, 1, :, tail]
         self.c = copy(sc, rc, 0, p.at(c=1 - p.c))
         self.y = copy(self.sy, ry, 1, p.at(y=1 - p.y))
         self.z = [copy(self.sz[k], rz.at[k], 2 + k, p.at(z=p.z_partner(k))) for k in range(3)]
         self.x = copy(self.sx, rx, 5, p.at(x=1 - p.x))
 
+    @staticmethod
+    def half(at, keep, x):
+        return pl.ds(pl.multiple_of(at + x * keep, 128), keep)
+
     def start_c(self):
         sc, p = self.buffers[0], self.place
 
@@ -708,51 +728,72 @@
         lax.fori_loop(0, 4, body, 0)
         self.c.start()
 
+    def start_x1(self):
+        rc, p = self.buffers[1], self.place
+        self.c.wait()
+
+        def body(z, carry):
+            away = self.grad[z, :, p.c, :, self.away] + rc[z, :, :, self.local_away].astype(F32)
+            self.sx1[z] = away.astype(self.kind)
+            self.grad[z, :, p.c, :, self.part] += rc[z, :, :, self.local].astype(F32)
+            return carry
+
+        lax.fori_loop(0, 4, body, 0)
+        self.x1.start()
+
     def start_y(self):
-        rc, sy = self.buffers[1], self.sy
         p = self.place
-        self.c.wait()
+        if self.halved:
+            held = self.buffers[5]
+            self.x1.wait_recv()
+        else:
+            held = self.buffers[1]
+            self.c.wait()
 
         def body(z, carry):
-            away = self.grad[z, 1 - p.y, p.c, :, self.cols] + rc[z, 1 - p.y].astype(F32)
-            sy[z] = away.astype(self.kind)
-            self.grad[z, p.y, p.c, :, self.cols] += rc[z, p.y].astype(F32)
+            away = self.grad[z, 1 - p.y, p.c, :, self.part] + held[z, 1 - p.y].astype(F32)
+            self.sy[z] = away.astype(self.kind)
+            self.grad[z, p.y, p.c, :, self.part] += held[z, p.y].astype(F32)
             return carry
 
         lax.fori_loop(0, 4, body, 0)
         self.y.start()
 
     def start_z(self):
-        ry, sz = self.buffers[2], self.sz
-        p = self.place
+        ry, p = self.buffers[2], self.place
         self.y.wait_recv()
         for k in (2, 1, 0):
             owner = p.z_partner(k)
-            away = self.grad[owner, p.y, p.c, :, self.cols] + ry[owner].astype(F32)
-            sz[k][...] = away.astype(self.kind)
+            away = self.grad[owner, p.y, p.c, :, self.part] + ry[owner].astype(F32)
+            self.sz[k][...] = away.astype(self.kind)
             self.z[k].start()
-        self.grad[p.z, p.y, p.c, :, self.cols] += ry[p.z].astype(F32)
+        self.grad[p.z, p.y, p.c, :, self.part] += ry[p.z].astype(F32)
 
     def start_x(self):
-        rz, sx = self.buffers[3], self.sx
-        p = self.place
+        rz, p = self.buffers[3], self.place
         for copy in self.z:
             copy.wait_recv()
-        near = self.grad[p.z, p.y, p.c, :, self.cols] + rz[0].astype(F32)
-        sx[...] = (near + (rz[1].astype(F32) + rz[2].astype(F32))).astype(self.kind)
+        near = self.grad[p.z, p.y, p.c, :, self.part] + rz[0].astype(F32)
+        self.sx[...] = (near + (rz[1].astype(F32) + rz[2].astype(F32))).astype(self.kind)
         self.x.start()
 
     def finish(self, out):
-        sx, rx = self.sx, self.buffers[4]
+        rx = self.buffers[4]
         self.x.wait_recv()
-        out[:, self.cols] = sx[...].astype(F32) + rx[...].astype(F32)
+        if self.halved:
+            out[:, self.part] = self.sx[...].astype(F32)
+            out[:, self.away] = rx[...].astype(F32)
+        else:
+            out[:, self.cols] = self.sx[...].astype(F32) + rx[...].astype(F32)
 
     def close(self):
-        for copy in self.z + [self.y, self.x]:
+        for copy in self.z + [self.y, self.x] + ([self.x1] if self.halved else []):
             copy.wait_send()
 
 
-REDUCE_LEADS = ((4, 2), (4, 2), (4,), (3,), ())
+def reduce_leads(halved):
+    leads = [((4, 2), False), ((4, 2), False), ((4,), halved), ((3,), halved), ((), halved)]
+    return leads + ([((4, 2), True)] if halved else [])
 
 
 def layer_scratch(row_count, width, hidden_width, shards):
@@ -828,8 +869,9 @@
     plan = [(r.pack, r.pack_own, 0, 128)]
     plan += [(r.w_qkv, r.qkv_in, k * width, width) for k in range(3)]
     plan += [(r.w_out, r.out_in, 0, width)]
-    plan += [(r.w_up, r.up_in, k * hidden_width // 2, hidden_width // 2) for k in range(2)]
-    plan += [(r.w_down, r.down_in, k * width // 2, width // 2) for k in range(2)]
+    half = hidden_width // 2
+    plan += [(r.w_up, r.up_in, k * half, half, True) for k in range(2)]
+    plan += [(r.w_down, r.down_in, k * width // 2, width // 2, True) for k in range(2)]
     gathers = [Gather(r, place, k, *item) for k, item in enumerate(plan)]
     pack, q, k, v, out, up0, up1, down0, down1 = gathers
     pack.start_z()
@@ -864,18 +906,23 @@
             i,
             {
                 1: [out.start_y],
-                2: [out.start_c],
-                3: [up0.start_y],
-                5: [up1.start_y, up0.start_c],
-                7: [down0.start_y, up1.start_c],
-                9: [down1.start_y, down0.start_c],
+                3: [up0.start_y, out.start_c],
+                5: [up1.start_y, up0.start_x],
+                7: [down0.start_y, up1.start_x, up0.start_c],
+                9: [down1.start_y, down0.start_x, up1.start_c],
             },
         ),
     )
-    down1.start_c()
-    for group in (out, up0, up1, down0, down1):
-        group.ready()
-    middle_part(r, scale)
+    out.ready()
+
+    def arrive():
+        down1.start_x()
+        down0.start_c()
+        down1.start_c()
+        for group in (up0, up1, down0, down1):
+            group.ready()
+
+    middle_part(r, scale, arrive)
 
     plan = [(r.g_down,), (r.g_up,), (r.g_out,)]
     plan += [(r.g_qkv, k * width) for k in range(3)] + [(r.g_pack,)]
@@ -889,23 +936,24 @@
         lambda i: at_step(
             i,
             {
-                1: [down.start_y],
-                2: [up.start_y],
-                3: [out.start_y],
-                5: [down.start_z],
-                8: [up.start_z, down.start_x],
-                9: [out.start_z],
+                1: [down.start_y, up.start_x1],
+                2: [out.start_x1],
+                6: [down.start_z, up.start_y],
+                7: [out.start_y],
+                9: [up.start_z],
             },
         ),
     )
-    for third, group in enumerate((q, k, v)):
-        qkv_weight_grad(r, third)
-        group.start_c()
-        if third:
-            (q, k)[third - 1].start_y()
-    v.start_y()
-    up.start_x()
-    out.start_x()
+    qkv_weight_grad(r, 0)
+    q.start_c()
+    qkv_weight_grad(r, 2)
+    v.start_c()
+    q.start_y()
+    qkv_weight_grad(r, 1)
+    k.start_c()
+    v.start_x1()
+    out.start_z()
+    k.start_y()
 
     def stored(i):
         rows = pl.ds(pl.multiple_of(i * 4 * LENGTH, 4 * LENGTH), 4 * LENGTH)
@@ -916,18 +964,26 @@
     start_back(
         r,
         lambda i: at_step(
-            i, {2: [q.start_z], 4: [k.start_z], 6: [v.start_z, q.start_x], 8: [k.start_x]}
+            i,
+            {
+                2: [down.start_x],
+                3: [up.start_x, q.start_z],
+                5: [v.start_y, out.start_x],
+                6: [k.start_z],
+                8: [v.start_z, q.start_x],
+            },
         ),
         lambda i: stored(i).start(),
     )
     pack_grads(r)
     pack.start_c()
+    k.start_x()
     v.start_x()
     pack.start_y()
     down.finish(r.down_out)
     up.finish(r.up_out)
+    pack.start_z()
     out.finish(r.out_out)
-    pack.start_z()
     for group in (q, k, v):
         group.finish(r.qkv_out)
     pack.start_x()
@@ -985,7 +1041,7 @@
     load.wait()
     norm_pass(r)
     front(r, lambda i: None)
-    middle_part(r, scale)
+    middle_part(r, scale, lambda: None)
     attend_back(r, lambda i: None)
     for third in range(3):
         qkv_weight_grad(r, third)
@@ -1102,15 +1158,15 @@
             small=((8, width), F32),
             actor=((SLOTS, width), BF16),
             up_bias=((1, hidden_width), F32),
-            gather_send=pltpu.SemaphoreType.DMA((GATHERS, 5)),
-            gather_recv=pltpu.SemaphoreType.DMA((GATHERS, 5)),
-            reduce_send=pltpu.SemaphoreType.DMA((len(REDUCES), 6)),
-            reduce_recv=pltpu.SemaphoreType.DMA((len(REDUCES), 6)),
+            gather_send=pltpu.SemaphoreType.DMA((GATHERS, 6)),
+            gather_recv=pltpu.SemaphoreType.DMA((GATHERS, 6)),
+            reduce_send=pltpu.SemaphoreType.DMA((len(REDUCES), 7)),
+            reduce_recv=pltpu.SemaphoreType.DMA((len(REDUCES), 7)),
             store_sem=pltpu.SemaphoreType.DMA((row_count // (4 * LENGTH),)),
         )
-        for index, (count, rows, kind) in enumerate(REDUCES):
-            for item, lead in enumerate(REDUCE_LEADS):
-                scratch[index, item] = (lead + (rows, count), kind)
+        for index, (count, rows, kind, halved) in enumerate(REDUCES):
+            for item, (lead, half) in enumerate(reduce_leads(halved)):
+                scratch[index, item] = (lead + (rows, count // 2 if half else count), kind)
         tokens_grad, pack, qkv_g, out_g, up_g, down_g = run(
             spread_kernel, scale, ins, outs | shard_grads, scratch, flops, True, 0
         )

time: 218 us -> 210 us (0.963)
  Pallas kernels: 217 us -> 209 us
    pallas_call x2, Pallas kernels: 217 us -> 209 us  [run(): pl.pallas_call(functools.partial(kernel, (*ins, *outs, *scratch), constan...]
where the time goes in v2:
time: 210 us
  Pallas kernels  209 us (100%)
    pallas_call x2, Pallas kernels, run(): pl.pallas_call(functools.partial(kernel, (*ins, *outs, *scratch), constan...  209 us

profile of v2, /device:TPU:0, one launch (start us, length us, event | category | flops | bytes accessed | tf_op | source)
XLA Modules:
  0.0 210.2 jit_solution(5439651367989397123)
XLA Ops:
  0.7 202.4 %shard_map.358 = (f32[2560,512]{1,0:T(8,128)}, f32[40,128]{1,0:T(8,128)}, f32[32,1536]{1,0:T(8,128)}, f32[32,512]{1,0:T(8,128)}, f32[32,2048]{1,0:T(8,128)}, /*index=5*/f32[512,128]{1,0:T(8,128)}) custom-call(f32[2,26]{1,0:T(2,128)} %refs_0_.3, f32[2,26]{1,0:T(2,128)} %refs_1_.3, bf16[2560,512]{1,0:T(8,128)(2,1)} %refs_2_.1, bf16[18]{0:T(256)(128)(2,1)} %refs_3_.1, ...), custom_call_target="tpu_custom_call" | custom-call | flops 48318382080 | bytes 16777216 | tf_op jit(solution)/shard_map/pallas_call | solution.py:1059
  203.1 6.9 %shard_map.359 = (f32[1,1]{1,0:T(1,128)}, f32[2,26]{1,0:T(2,128)}, f32[32,64]{1,0:T(8,128)}, f32[32,1536]{1,0:T(8,128)}, f32[32,512]{1,0:T(8,128)}, /*index=5*/f...) custom-call(f32[2,26]{1,0:T(2,128)} %refs_0_.3, ...), custom_call_target="tpu_custom_call" | custom-call | bytes 16777216 | tf_op jit(solution)/shard_map/pallas_call | solution.py:1059

commit v3 on v2

--- a/solution.py
+++ b/solution.py
@@ -122,23 +122,21 @@
 def attend_group(r, i):
     masks, bias = pair_masks(), r.causal[...]
     group = chains(r, i)
-    scores = [
-        dot(r.qkv[rows, k], spread_heads(r.qkv[rows, q], masks), 1, 1)
-        for _, rows, (q, k, _) in group
-    ]
-    probs = []
-    for (seq, _, (q, _, _)), score in zip(group, scores, strict=True):
+    loaded = [[r.qkv[rows, part] for part in parts] for _, rows, parts in group]
+    scores = [dot(key, spread_heads(query, masks), 1, 1) for query, key, _ in loaded]
+    probs, totals = [], []
+    for score in scores:
         score = score * SCORE_SCALE + bias
         highest = jnp.max(score, 0, keepdims=True)
         weights = jnp.exp2(score - highest)
         summed = jnp.sum(weights, 0, keepdims=True)
         probs.append((weights * (1.0 / summed)).astype(BF16))
-        r.totals[pl.ds(seq, 1), q] = highest + jnp.log(summed) * LOG2E
-    blocks = [
-        dot(prob, r.qkv[rows, v], 0, 0) for (_, rows, (_, _, v)), prob in zip(group, probs, strict=True)
-    ]
-    for (_, rows, (q, _, _)), block in zip(group, blocks, strict=True):
-        r.attended[rows, q] = gather_heads(block).astype(BF16)
+        totals.append(highest + jnp.log(summed) * LOG2E)
+    blocks = [dot(prob, value, 0, 0) for prob, (_, _, value) in zip(probs, loaded, strict=True)]
+    done = [gather_heads(block).astype(BF16) for block in blocks]
+    for (seq, rows, (q, _, _)), result, total in zip(group, done, totals, strict=True):
+        r.attended[rows, q] = result
+        r.totals[pl.ds(seq, 1), q] = total
 
 
 def attend_back_group(r, i):
@@ -221,10 +219,14 @@
     return block.reshape(-1, block.shape[-1])
 
 
-def start_rows(r, row, at):
-    frame = at % LENGTH
-    start = r.tokens[pl.ds(pl.multiple_of(row + at, STRIP), STRIP), :].astype(F32)
-    return start + r.positions[frame : frame + STRIP, :]
+def strip_rows(row, count):
+    return [pl.ds(pl.multiple_of(row + at, STRIP), STRIP) for at in range(0, count, STRIP)]
+
+
+def load_starts(r, row, count):
+    starts = [r.tokens[rows, :].astype(F32) for rows in strip_rows(row, count)]
+    frames = [r.positions[at : at + STRIP, :] for at in range(0, LENGTH, STRIP)]
+    return [start + frames[k % len(frames)] for k, start in enumerate(starts)]
 
 
 def norm_pass(r):
@@ -233,32 +235,42 @@
 
     def body(i, carry):
         row = pl.multiple_of(i * rows, rows)
-        for at in range(0, rows, STRIP):
-            unit, _ = normalise(start_rows(r, row, at))
-            normed = unit * r.small[G1 : G1 + 1, :] + r.small[B1 : B1 + 1, :]
-            r.attended[pl.ds(pl.multiple_of(row + at, STRIP), STRIP), :] = normed.astype(BF16)
-        r.normed_t[:, pl.ds(row, rows)] = r.attended[pl.ds(row, rows), :].T
+        normed = [
+            (normalise(start)[0] * r.small[G1 : G1 + 1, :] + r.small[B1 : B1 + 1, :]).astype(BF16)
+            for start in load_starts(r, row, rows)
+        ]
+        normed = jnp.concatenate(normed, 0)
+        turned = normed.T
+        r.attended[pl.ds(row, rows), :] = normed
+        r.normed_t[:, pl.ds(row, rows)] = turned
         return carry
 
     lax.fori_loop(0, count // rows, body, 0)
 
 
+def project_third(r, third):
+    count, width = r.tokens.shape
+    rows = 8 * LENGTH
+    columns = slice(third * width, (third + 1) * width)
+
+    def body(i, carry):
+        here = pl.ds(pl.multiple_of(i * rows, rows), rows)
+        weight = merged(r.w_qkv[:, :, :, :, columns])
+        r.qkv[here, columns] = dot(r.attended[here, :], weight, 1, 0).astype(BF16)
+        return carry
+
+    lax.fori_loop(0, count // rows, body, 0)
+
+
 def front(r, pump):
-    count, width = r.tokens.shape
-    rows = 4 * LENGTH
+    count = r.tokens.shape[0]
 
     def body(i, carry):
         pump(i)
-        row = pl.multiple_of(i * rows, rows)
-        normed = r.attended[pl.ds(row, rows), :]
-        for at in range(0, 3 * width, width):
-            r.qkv[pl.ds(row, rows), at : at + width] = dot(
-                normed, merged(r.w_qkv[:, :, :, :, at : at + width]), 1, 0
-            ).astype(BF16)
         attend_group(r, i)
         return carry
 
-    lax.fori_loop(0, count // rows, body, 0)
+    lax.fori_loop(0, count // (4 * LENGTH), body, 0)
 
 
 def add_grad(ref, index, values):
@@ -331,13 +343,12 @@
     def tile_rows(i):
         return pl.ds(pl.multiple_of(i * rows, rows), rows)
 
-    def project(i):
-        return dot(r.attended[tile_rows(i), :], merged(out_weight[...]), 1, 0)
-
-    def before(i, t, projected):
-        row = pl.multiple_of(i * rows, rows)
-        for strip in strips:
-            mid = start_rows(r, row, strip.start) + projected[strip]
+    def before(t, tokens, attended):
+        projected = dot(attended, merged(out_weight[...]), 1, 0)
+        for k, strip in enumerate(strips):
+            frame = k * STRIP % LENGTH
+            start = tokens[k].astype(F32) + r.positions[frame : frame + STRIP, :]
+            mid = start + projected[strip]
             unit, spread = normalise(mid)
             r.two_low[strip, :] = (unit * gain(G2) + gain(B2)).astype(BF16)
             t.unit[strip, :] = unit
@@ -351,55 +362,61 @@
     def up_weight(j):
         return merged(r.w_up[:, :, :, :, columns(j)])
 
-    def activate(j, t, hidden):
+    def activate(hidden, bias):
+        done = [gelu_pair(hidden[at : at + THIN] + bias) for at in range(0, rows, THIN)]
+        values = jnp.concatenate([value.astype(BF16) for value, _ in done], 0)
+        return values, jnp.concatenate([slope.astype(BF16) for _, slope in done], 0)
+
+    def forward_only(j, t):
         cols = columns(j)
-        bias = r.up_bias[:, cols]
-        for at in range(0, rows, THIN):
-            value, derivative = gelu_pair(hidden[at : at + THIN] + bias)
-            t.active[at : at + THIN, cols] = value.astype(BF16)
-            t.slope[at : at + THIN, cols] = derivative.astype(BF16)
-
-    def forward_only(j, t):
-        activate(j, t, dot(r.two_low[...], up_weight(j), 1, 0))
-        t.last[...] += dot(t.active[:, columns(j)], merged(r.w_down[j]), 1, 0)
+        weight, bias, down = up_weight(j), r.up_bias[:, cols], merged(r.w_down[j])
+        active, slope = activate(dot(r.two_low[...], weight, 1, 0), bias)
+        t.last[...] += dot(active, down, 1, 0)
+        t.active[:, cols], t.slope[:, cols] = active, slope
 
     def both_ways(j, here, there):
         cols = columns(j)
+        bias, total = r.up_bias[:, cols], r.g_up_bias[:, cols]
         if there is not None:
             hidden = dot(r.two_low[...], up_weight(j), 1, 0)
-        hidden_grad = dot(r.low[...], merged(r.w_down[j]), 1, 1)
-        add_columns(r.g_down.at[j], dot(r.low_t[...], here.active[:, cols], 1, 0))
-        total = r.g_up_bias[:, cols]
+        above = dot(r.low[...], merged(r.w_down[j]), 1, 1)
         for at in range(0, rows, THIN):
             strip = slice(at, at + THIN)
-            part = (hidden_grad[strip] * here.slope[strip, cols].astype(F32)).astype(BF16)
+            part = (above[strip] * here.slope[strip, cols].astype(F32)).astype(BF16)
             r.hidden_grad[strip, :] = part
             total += fold_rows(part.astype(F32))
-        r.g_up_bias[:, cols] = total
+        add_columns(r.g_down.at[j], dot(r.low_t[...], here.active[:, cols], 1, 0))
         r.two_in[...] += dot(r.hidden_grad[...], up_weight(j), 1, 1)
         add_grad(
             r.g_up,
             (everything, everything, everything, everything, cols),
             dot(here.two_t[...], r.hidden_grad[...], 1, 0),
         )
+        r.g_up_bias[:, cols] = total
         if there is not None:
-            activate(j, there, hidden)
-            there.last[...] += dot(there.active[:, cols], merged(r.w_down[j]), 1, 0)
-
-    def last_norm(i, t):
+            active, slope = activate(hidden, bias)
+            there.last[...] += dot(active, merged(r.w_down[j]), 1, 0)
+            there.active[:, cols], there.slope[:, cols] = active, slope
+
+    def chunks(step):
+        def body(j, carry):
+            step(j)
+            return carry
+
+        lax.fori_loop(0, shards, body, 0)
+
+    def last_norm(t):
+        spreads = []
         for strip in strips:
             unit, spread = normalise(t.last[strip, :])
             r.low[strip, :] = (unit * gain(GL) + gain(BL)).astype(BF16)
             t.last[strip, :] = unit
-            r.scale_last[strip, :] = spread
-        return dot(r.actor[...], r.low[...], 1, 1) + head_bias
-
-    def head(i, logits):
-        here = tile_rows(i)
-        masks = jnp.concatenate(
-            [r.masks[:, here], jnp.zeros((SLOTS - slots, rows), jnp.int32)], 0
-        )
-        loss, pull = policy(logits, masks, r.action_row[:, here], r.advantage[:, here], scale)
+            spreads.append(spread)
+        return spreads, dot(r.actor[...], r.low[...], 1, 1) + head_bias
+
+    def head(logits, masks, actions, advantage):
+        masks = jnp.concatenate([masks, jnp.zeros((SLOTS - slots, rows), jnp.int32)], 0)
+        loss, pull = policy(logits, masks, actions, advantage, scale)
         logit_grad = pull.astype(BF16)
         last_in = dot(logit_grad, r.actor[...], 0, 0)
         r.g_actor[...] += dot(logit_grad, r.low[...], 1, 0)
@@ -414,11 +431,11 @@
         r.head_sums[SLOTS : SLOTS + 1, :] = fold
         return last_in
 
-    def last_norm_back(t, last_in):
+    def last_norm_back(t, spreads, last_in):
         sums = [r.g_small[k] for k in (GL, BL, DB)]
-        for strip in strips:
+        for strip, spread in zip(strips, spreads, strict=True):
             above, unit = last_in[strip], t.last[strip, :]
-            grad = norm_back(unit, r.scale_last[strip, :], gain(GL), above)
+            grad = norm_back(unit, spread, gain(GL), above)
             sums[0] += fold_rows(above * unit)
             sums[1] += fold_rows(above)
             sums[2] += fold_rows(grad)
@@ -429,49 +446,51 @@
         r.low_t[...] = r.low[...].T
         r.two_in[...] = jnp.zeros((rows, width), F32)
 
-    def two_norm_back(i, t):
-        row = pl.multiple_of(i * rows, rows)
+    def two_norm_back(t):
         sums = [r.g_small[k] for k in (G2, B2)]
         for strip in strips:
             above, unit = r.two_in[strip, :], t.unit[strip, :]
             sums[0] += fold_rows(above * unit)
             sums[1] += fold_rows(above)
             grad = t.last[strip, :] + norm_back(unit, t.scale[strip, :], gain(G2), above)
-            r.middle_grad[pl.ds(pl.multiple_of(row + strip.start, STRIP), STRIP), :] = grad
-            r.middle_low[strip, :] = grad.astype(BF16)
+            t.last[strip, :] = grad
+            r.hidden_grad[strip, :] = grad.astype(BF16)
         for k, total in zip((G2, B2), sums, strict=True):
             r.g_small[k] = total
 
-    def out_back(i):
-        here = tile_rows(i)
-        add_grad(r.g_out, ..., dot(r.attended[here, :], r.middle_low[...], 0, 0))
-        r.attended[here, :] = dot(r.middle_low[...], merged(out_weight[...]), 1, 1).astype(BF16)
+    def out_back(i, t, attended):
+        low = r.hidden_grad[...]
+        add_grad(r.g_out, ..., dot(attended, low, 0, 0))
+        r.attended[tile_rows(i), :] = dot(low, merged(out_weight[...]), 1, 1).astype(BF16)
+        r.middle_grad[tile_rows(i), :] = t.last[...]
 
     sides = [Tile(r, 0), Tile(r, 1)]
     tiles = count // rows
 
-    def chunks(step):
-        def body(j, carry):
-            step(j)
-            return carry
-
-        lax.fori_loop(0, shards, body, 0)
+    def begin(i):
+        row = pl.multiple_of(i * rows, rows)
+        return [r.tokens[part, :] for part in strip_rows(row, rows)], r.attended[tile_rows(i), :]
 
     def step(i, side, first=False, last=False):
         here, there = sides[side], sides[1 - side]
-        projected = None if last else project(i + 1)
-        logits = last_norm(i, here)
+        at = tile_rows(i)
+        side_data = r.masks[:, at], r.action_row[:, at], r.advantage[:, at]
         if not first:
-            two_norm_back(i - 1, there)
-        last_in = head(i, logits)
+            attended = r.attended[tile_rows(i - 1), :]
         if not last:
-            before(i + 1, there, projected)
-        last_norm_back(here, last_in)
+            ahead = begin(i + 1)
+        spreads, logits = last_norm(here)
         if not first:
-            out_back(i - 1)
+            two_norm_back(there)
+        last_in = head(logits, *side_data)
+        if not first:
+            out_back(i - 1, there, attended)
+        last_norm_back(here, spreads, last_in)
+        if not last:
+            before(there, *ahead)
         chunks(lambda j: both_ways(j, here, None if last else there))
 
-    before(0, sides[0], project(0))
+    before(sides[0], *begin(0))
     arrive()
     chunks(lambda j: forward_only(j, sides[0]))
     step(0, 0, first=True)
@@ -483,8 +502,8 @@
 
     lax.fori_loop(0, (tiles - 2) // 2, pair, 0)
     step(tiles - 1, 1, last=True)
-    two_norm_back(tiles - 1, sides[1])
-    out_back(tiles - 1)
+    two_norm_back(sides[1])
+    out_back(tiles - 1, sides[1], r.attended[tile_rows(tiles - 1), :])
 
 
 def attend_back(r, pump):
@@ -504,7 +523,8 @@
     step = width // 2
     for at in range(third * width, (third + 1) * width, step):
         values = dot(r.normed_t[...], r.qkv[:, at : at + step], 1, 0)
-        r.g_qkv[:, :, :, :, at : at + step] = values.reshape(r.g_qkv.shape[:4] + (step,))
+        values = values.astype(BF16).reshape(r.g_qkv.shape[:4] + (step,))
+        r.g_qkv[:, :, :, :, at : at + step] = values
 
 
 def start_back(r, pump, tile_done):
@@ -515,20 +535,22 @@
     def body(i, carry):
         pump(i)
         row = pl.multiple_of(i * rows, rows)
+        starts = load_starts(r, row, rows)
         one_in = dot(r.qkv[pl.ds(row, rows), :], merged(r.w_qkv[...]), 1, 1)
         sums = [r.g_small[k] for k in (G1, B1)]
-        for at in range(0, rows, STRIP):
-            there = pl.ds(pl.multiple_of(row + at, STRIP), STRIP)
-            unit, scale = normalise(start_rows(r, row, at))
-            above = one_in[at : at + STRIP]
+        frames = [r.g_positions[at : at + STRIP, :] for at in range(0, LENGTH, STRIP)]
+        grads = []
+        for k, (start, there) in enumerate(zip(starts, strip_rows(row, rows), strict=True)):
+            unit, scale = normalise(start)
+            above = one_in[k * STRIP : (k + 1) * STRIP]
             sums[0] += fold_rows(above * unit)
             sums[1] += fold_rows(above)
-            grad = r.middle_grad[there, :] + norm_back(unit, scale, gain, above)
-            r.middle_grad[there, :] = grad
-            frame = at % LENGTH
-            r.g_positions[frame : frame + STRIP, :] += grad
+            grads.append(r.middle_grad[there, :] + norm_back(unit, scale, gain, above))
+            frames[k % len(frames)] += grads[k]
+        r.g_positions[...] = jnp.concatenate(frames, 0)
         for k, total in zip((G1, B1), sums, strict=True):
             r.g_small[k] = total
+        r.middle_grad[pl.ds(row, rows), :] = jnp.concatenate(grads, 0)
         tile_done(i)
         return carry
 
@@ -718,6 +740,10 @@
     def half(at, keep, x):
         return pl.ds(pl.multiple_of(at + x * keep, 128), keep)
 
+    def add(self, index, values):
+        total = self.grad[index].astype(F32) + values.astype(F32)
+        self.grad[index] = total.astype(self.grad.dtype)
+
     def start_c(self):
         sc, p = self.buffers[0], self.place
 
@@ -733,9 +759,9 @@
         self.c.wait()
 
         def body(z, carry):
-            away = self.grad[z, :, p.c, :, self.away] + rc[z, :, :, self.local_away].astype(F32)
+            away = self.grad[z, :, p.c, :, self.away].astype(F32) + rc[z, :, :, self.local_away].astype(F32)
             self.sx1[z] = away.astype(self.kind)
-            self.grad[z, :, p.c, :, self.part] += rc[z, :, :, self.local].astype(F32)
+            self.add((z, slice(None), p.c, slice(None), self.part), rc[z, :, :, self.local])
             return carry
 
         lax.fori_loop(0, 4, body, 0)
@@ -751,9 +777,9 @@
             self.c.wait()
 
         def body(z, carry):
-            away = self.grad[z, 1 - p.y, p.c, :, self.part] + held[z, 1 - p.y].astype(F32)
+            away = self.grad[z, 1 - p.y, p.c, :, self.part].astype(F32) + held[z, 1 - p.y].astype(F32)
             self.sy[z] = away.astype(self.kind)
-            self.grad[z, p.y, p.c, :, self.part] += held[z, p.y].astype(F32)
+            self.add((z, p.y, p.c, slice(None), self.part), held[z, p.y])
             return carry
 
         lax.fori_loop(0, 4, body, 0)
@@ -764,16 +790,16 @@
         self.y.wait_recv()
         for k in (2, 1, 0):
             owner = p.z_partner(k)
-            away = self.grad[owner, p.y, p.c, :, self.part] + ry[owner].astype(F32)
+            away = self.grad[owner, p.y, p.c, :, self.part].astype(F32) + ry[owner].astype(F32)
             self.sz[k][...] = away.astype(self.kind)
             self.z[k].start()
-        self.grad[p.z, p.y, p.c, :, self.part] += ry[p.z].astype(F32)
+        self.add((p.z, p.y, p.c, slice(None), self.part), ry[p.z])
 
     def start_x(self):
         rz, p = self.buffers[3], self.place
         for copy in self.z:
             copy.wait_recv()
-        near = self.grad[p.z, p.y, p.c, :, self.part] + rz[0].astype(F32)
+        near = self.grad[p.z, p.y, p.c, :, self.part].astype(F32) + rz[0].astype(F32)
         self.sx[...] = (near + (rz[1].astype(F32) + rz[2].astype(F32))).astype(self.kind)
         self.x.start()
 
@@ -821,10 +847,8 @@
         two_low=((tile, width), BF16),
         low=((tile, width), BF16),
         low_t=((width, tile), BF16),
-        middle_low=((tile, width), BF16),
+        two_in=((tile, width), F32),
         hidden_grad=((tile, hidden_width // 4), BF16),
-        two_in=((tile, width), F32),
-        scale_last=((tile, 1), F32),
         local_sem=pltpu.SemaphoreType.DMA((2,)),
     )
 
@@ -833,7 +857,7 @@
     split = SPLIT
     part, hidden_part = width // shards, hidden_width // shards
     return dict(
-        g_qkv=(split + (part, 3 * width), F32),
+        g_qkv=(split + (part, 3 * width), BF16),
         g_out=(split + (part, width), F32),
         g_up=(split + (part, hidden_width), F32),
         g_down=(split + (width, hidden_part), F32),
@@ -881,7 +905,6 @@
     pack.start_y()
     q.start_y()
     pack.start_c()
-    clear(r)
     frame_values(r)
     pack.ready()
     unpack_shards(r)
@@ -896,9 +919,14 @@
     up1.start_z()
     down0.start_z()
     down1.start_z()
+    q.ready()
+    project_third(r, 0)
     v.start_c()
-    for group in (q, k, v):
-        group.ready()
+    clear(r)
+    k.ready()
+    project_third(r, 1)
+    v.ready()
+    project_third(r, 2)
 
     front(
         r,
@@ -1040,6 +1068,8 @@
     frame_values(r)
     load.wait()
     norm_pass(r)
+    for third in range(3):
+        project_third(r, third)
     front(r, lambda i: None)
     middle_part(r, scale, lambda: None)
     attend_back(r, lambda i: None)
@@ -1244,7 +1274,8 @@
 
     down_sum = jnp.swapaxes(sums.g_down, 3, 4)
     qkv_part, out_part, up_part, down_part = (
-        scatter(merged(grad), 0) for grad in (sums.g_qkv, sums.g_out, sums.g_up, down_sum)
+        scatter(merged(grad).astype(F32), 0)
+        for grad in (sums.g_qkv, sums.g_out, sums.g_up, down_sum)
     )
     rows = [jnp.sum(sums.g_small, 1), sums.g_actor[:slots], sums.g_positions]
     side = scatter(jnp.concatenate(rows, 0), 1)

time: 210 us -> 201 us (0.957)
  Pallas kernels: 209 us -> 200 us
    pallas_call x2, Pallas kernels: 209 us -> 200 us  [run(): pl.pallas_call(functools.partial(kernel, (*ins, *outs, *scratch), constan...]
where the time goes in v3:
time: 201 us
  Pallas kernels  200 us (100%)
    pallas_call x2, Pallas kernels, run(): pl.pallas_call(functools.partial(kernel, (*ins, *outs, *scratch), constan...  200 us

profile of v3, /device:TPU:0, one launch (start us, length us, event | category | flops | bytes accessed | tf_op | source)
XLA Modules:
  0.0 201.2 jit_solution(5921269550247246140)
XLA Ops:
  0.7 193.4 %shard_map.358 = (f32[2560,512]{1,0:T(8,128)}, f32[40,128]{1,0:T(8,128)}, f32[32,1536]{1,0:T(8,128)}, f32[32,512]{1,0:T(8,128)}, f32[32,2048]{1,0:T(8,128)}, /*index=5*/f32[512,128]{1,0:T(8,128)}) custom-call(f32[2,26]{1,0:T(2,128)} %refs_0_.3, f32[2,26]{1,0:T(2,128)} %refs_1_.3, bf16[2560,512]{1,0:T(8,128)(2,1)} %refs_2_.1, bf16[18]{0:T(256)(128)(2,1)} %refs_3_.1, ...), custom_call_target="tpu_custom_call" | custom-call | flops 48318382080 | bytes 16777216 | tf_op jit(solution)/shard_map/pallas_call | solution.py:1089
  194.1 6.9 %shard_map.359 = (f32[1,1]{1,0:T(1,128)}, f32[2,26]{1,0:T(2,128)}, f32[32,64]{1,0:T(8,128)}, f32[32,1536]{1,0:T(8,128)}, f32[32,512]{1,0:T(8,128)}, /*index=5*/f...) custom-call(f32[2,26]{1,0:T(2,128)} %refs_0_.3, ...), custom_call_target="tpu_custom_call" | custom-call | bytes 16777216 | tf_op jit(solution)/shard_map/pallas_call | solution.py:1089

commit v4 on v3

--- a/solution.py
+++ b/solution.py
@@ -643,6 +643,9 @@
     def z_partner(self, k):
         return (self.z + 1 - 2 * (self.z % 2), (self.z + 2) % 4, 3 - self.z)[k]
 
+    def lines(self):
+        return [self.z] + [self.z_partner(k) for k in range(3)]
+
     def partners(self):
         return [self.at(z=self.z_partner(k)) for k in range(3)] + [
             self.at(y=1 - self.y),
@@ -672,40 +675,55 @@
         cols = part = slice(at, at + count)
         if halved:
             part = pl.ds(pl.multiple_of(at + p.x * (count // 2), 128), count // 2)
-        self.full, self.own, self.part, self.place = full, own, part, place
+        self.full, self.own, self.part, self.place, self.halved = full, own, part, place, halved
         mine = full.at[p.z, p.y, p.c, :, part]
         self.z = [copy(own.at[:, part], mine, k, p.at(z=p.z_partner(k))) for k in range(3)]
-        line = full.at[:, p.y, p.c, :, part]
-        self.y = copy(line, line, 3, p.at(y=1 - p.y))
-        plane = full.at[:, :, p.c, :, part]
-        self.x = copy(plane, plane, 4, p.at(x=1 - p.x)) if halved else None
-        plane = full.at[:, :, p.c, :, cols]
-        self.c = copy(plane, plane, 5, p.at(c=1 - p.c))
+        self.y, self.x, self.near, self.far = [], [], [], []
+        for k, z in enumerate(p.lines()):
+            shard = full.at[z, p.y, p.c, :, part]
+            self.y.append(copy(shard, shard, 3 + k, p.at(y=1 - p.y)))
+            if halved:
+                pair = full.at[z, :, p.c, :, part]
+                self.x.append(copy(pair, pair, 7 + k, p.at(x=1 - p.x)))
+                pair = full.at[z, :, p.c, :, cols]
+                self.far.append(copy(pair, pair, 11 + k, p.at(c=1 - p.c)))
+            else:
+                self.near.append(copy(shard, shard, 7 + k, p.at(c=1 - p.c)))
+                shard = full.at[z, 1 - p.y, p.c, :, part]
+                self.far.append(copy(shard, shard, 11 + k, p.at(c=1 - p.c)))
 
     def start_z(self):
         for copy in self.z:
             copy.start()
         p = self.place
         self.full[p.z, p.y, p.c, :, self.part] = self.own[:, self.part]
+        self.y[0].start()
+        if not self.halved:
+            self.near[0].start()
 
     def start_y(self):
-        for copy in self.z:
+        for k, copy in enumerate(self.z):
             copy.wait_recv()
-        self.y.start()
+            self.y[k + 1].start()
+            if not self.halved:
+                self.near[k + 1].start()
 
     def start_x(self):
-        self.y.wait_recv()
-        self.x.start()
+        for arrived, copy in zip(self.y, self.x, strict=True):
+            arrived.wait_recv()
+            copy.start()
 
     def start_c(self):
-        (self.y if self.x is None else self.x).wait_recv()
-        self.c.start()
+        for arrived, copy in zip(self.x if self.halved else self.y, self.far, strict=True):
+            arrived.wait_recv()
+            copy.start()
 
     def ready(self):
-        self.c.wait_recv()
+        for copy in self.near + self.far:
+            copy.wait_recv()
 
     def close(self):
-        for copy in self.z + [self.y, self.c] + ([] if self.x is None else [self.x]):
+        for copy in self.z + self.y + self.x + self.near + self.far:
             copy.wait_send()
 
 
@@ -720,21 +738,28 @@
         sc, rc, ry, rz, rx = self.buffers[:5]
         keep = count
         self.part = self.cols
+        self.lines = p.lines()
         if halved:
             keep = count // 2
             self.part = self.half(at, keep, p.x)
             self.away = self.half(at, keep, 1 - p.x)
             self.local, self.local_away = self.half(0, keep, p.x), self.half(0, keep, 1 - p.x)
+            held = self.buffers[5]
             self.sx1 = sc.at[:, :, :, 0:keep]
-            self.x1 = copy(self.sx1, self.buffers[5], 6, p.at(x=1 - p.x))
+            self.x1 = [
+                copy(self.sx1.at[z], held.at[z], 12 + k, p.at(x=1 - p.x))
+                for k, z in enumerate(self.lines)
+            ]
         tail = slice(count - keep, count)
         self.sy = sc.at[:, 0, :, tail]
         self.sz = [sc.at[k, 1, :, tail] for k in range(3)]
         self.sx = sc.at[3, 1, :, tail]
-        self.c = copy(sc, rc, 0, p.at(c=1 - p.c))
-        self.y = copy(self.sy, ry, 1, p.at(y=1 - p.y))
-        self.z = [copy(self.sz[k], rz.at[k], 2 + k, p.at(z=p.z_partner(k))) for k in range(3)]
-        self.x = copy(self.sx, rx, 5, p.at(x=1 - p.x))
+        self.c, self.y = [], []
+        for k, z in enumerate(self.lines):
+            self.c.append(copy(sc.at[z], rc.at[z], k, p.at(c=1 - p.c)))
+            self.y.append(copy(self.sy.at[z], ry.at[z], 4 + k, p.at(y=1 - p.y)))
+        self.z = [copy(self.sz[k], rz.at[k], 8 + k, p.at(z=p.z_partner(k))) for k in range(3)]
+        self.x = copy(self.sx, rx, 11, p.at(x=1 - p.x))
 
     @staticmethod
     def half(at, keep, x):
@@ -746,53 +771,43 @@
 
     def start_c(self):
         sc, p = self.buffers[0], self.place
-
-        def body(z, carry):
+        for z, copy in zip(self.lines, self.c, strict=True):
             sc[z] = self.grad[z, :, 1 - p.c, :, self.cols].astype(self.kind)
-            return carry
-
-        lax.fori_loop(0, 4, body, 0)
-        self.c.start()
+            copy.start()
 
     def start_x1(self):
         rc, p = self.buffers[1], self.place
-        self.c.wait()
-
-        def body(z, carry):
-            away = self.grad[z, :, p.c, :, self.away].astype(F32) + rc[z, :, :, self.local_away].astype(F32)
+        for z, arrived, copy in zip(self.lines, self.c, self.x1, strict=True):
+            arrived.wait()
+            away = self.grad[z, :, p.c, :, self.away].astype(F32)
+            away += rc[z, :, :, self.local_away].astype(F32)
             self.sx1[z] = away.astype(self.kind)
+            copy.start()
             self.add((z, slice(None), p.c, slice(None), self.part), rc[z, :, :, self.local])
-            return carry
-
-        lax.fori_loop(0, 4, body, 0)
-        self.x1.start()
 
     def start_y(self):
         p = self.place
-        if self.halved:
-            held = self.buffers[5]
-            self.x1.wait_recv()
-        else:
-            held = self.buffers[1]
-            self.c.wait()
-
-        def body(z, carry):
-            away = self.grad[z, 1 - p.y, p.c, :, self.part].astype(F32) + held[z, 1 - p.y].astype(F32)
+        held = self.buffers[5 if self.halved else 1]
+        for k, z in enumerate(self.lines):
+            if self.halved:
+                self.x1[k].wait_recv()
+            else:
+                self.c[k].wait()
+            away = self.grad[z, 1 - p.y, p.c, :, self.part].astype(F32)
+            away += held[z, 1 - p.y].astype(F32)
             self.sy[z] = away.astype(self.kind)
+            self.y[k].start()
             self.add((z, p.y, p.c, slice(None), self.part), held[z, p.y])
-            return carry
-
-        lax.fori_loop(0, 4, body, 0)
-        self.y.start()
 
     def start_z(self):
         ry, p = self.buffers[2], self.place
-        self.y.wait_recv()
-        for k in (2, 1, 0):
-            owner = p.z_partner(k)
+        for k in range(3):
+            owner = self.lines[k + 1]
+            self.y[k + 1].wait_recv()
             away = self.grad[owner, p.y, p.c, :, self.part].astype(F32) + ry[owner].astype(F32)
             self.sz[k][...] = away.astype(self.kind)
             self.z[k].start()
+        self.y[0].wait_recv()
         self.add((p.z, p.y, p.c, slice(None), self.part), ry[p.z])
 
     def start_x(self):
@@ -813,7 +828,7 @@
             out[:, self.cols] = self.sx[...].astype(F32) + rx[...].astype(F32)
 
     def close(self):
-        for copy in self.z + [self.y, self.x] + ([self.x1] if self.halved else []):
+        for copy in self.z + self.y + [self.x] + (self.x1 if self.halved else []):
             copy.wait_send()
 
 
@@ -906,22 +921,19 @@
     q.start_y()
     pack.start_c()
     frame_values(r)
+    k.start_y()
     pack.ready()
     unpack_shards(r)
-    k.start_y()
+    v.start_y()
     q.start_c()
     load.wait()
-    out.start_z()
-    up0.start_z()
     norm_pass(r)
-    v.start_y()
     k.start_c()
-    up1.start_z()
-    down0.start_z()
-    down1.start_z()
+    v.start_c()
+    for group in (out, up0, up1, down0, down1):
+        group.start_z()
     q.ready()
     project_third(r, 0)
-    v.start_c()
     clear(r)
     k.ready()
     project_third(r, 1)
@@ -1188,10 +1200,10 @@
             small=((8, width), F32),
             actor=((SLOTS, width), BF16),
             up_bias=((1, hidden_width), F32),
-            gather_send=pltpu.SemaphoreType.DMA((GATHERS, 6)),
-            gather_recv=pltpu.SemaphoreType.DMA((GATHERS, 6)),
-            reduce_send=pltpu.SemaphoreType.DMA((len(REDUCES), 7)),
-            reduce_recv=pltpu.SemaphoreType.DMA((len(REDUCES), 7)),
+            gather_send=pltpu.SemaphoreType.DMA((GATHERS, 15)),
+            gather_recv=pltpu.SemaphoreType.DMA((GATHERS, 15)),
+            reduce_send=pltpu.SemaphoreType.DMA((len(REDUCES), 16)),
+            reduce_recv=pltpu.SemaphoreType.DMA((len(REDUCES), 16)),
             store_sem=pltpu.SemaphoreType.DMA((row_count // (4 * LENGTH),)),
         )
         for index, (count, rows, kind, halved) in enumerate(REDUCES):

time: 201 us -> 195 us (0.970)
  Pallas kernels: 200 us -> 194 us
    pallas_call x2, Pallas kernels: 200 us -> 194 us  [run(): pl.pallas_call(functools.partial(kernel, (*ins, *outs, *scratch), constan...]
where the time goes in v4:
time: 195 us
  Pallas kernels  194 us (99%)
    pallas_call x2, Pallas kernels, run(): pl.pallas_call(functools.partial(kernel, (*ins, *outs, *scratch), constan...  194 us

profile of v4, /device:TPU:0, one launch (start us, length us, event | category | flops | bytes accessed | tf_op | source)
XLA Modules:
  0.0 194.7 jit_solution(8747392810365661757)
XLA Ops:
  0.7 187.0 %shard_map.358 = (f32[2560,512]{1,0:T(8,128)}, f32[40,128]{1,0:T(8,128)}, f32[32,1536]{1,0:T(8,128)}, f32[32,512]{1,0:T(8,128)}, f32[32,2048]{1,0:T(8,128)}, /*index=5*/f32[512,128]{1,0:T(8,128)}) custom-call(f32[2,26]{1,0:T(2,128)} %refs_0_.3, f32[2,26]{1,0:T(2,128)} %refs_1_.3, bf16[2560,512]{1,0:T(8,128)(2,1)} %refs_2_.1, bf16[18]{0:T(256)(128)(2,1)} %refs_3_.1, ...), custom_call_target="tpu_custom_call" | custom-call | flops 48318382080 | bytes 16777216 | tf_op jit(solution)/shard_map/pallas_call | solution.py:1101
  187.6 6.9 %shard_map.359 = (f32[1,1]{1,0:T(1,128)}, f32[2,26]{1,0:T(2,128)}, f32[32,64]{1,0:T(8,128)}, f32[32,1536]{1,0:T(8,128)}, f32[32,512]{1,0:T(8,128)}, /*index=5*/f...) custom-call(f32[2,26]{1,0:T(2,128)} %refs_0_.3, ...), custom_call_target="tpu_custom_call" | custom-call | bytes 16777216 | tf_op jit(solution)/shard_map/pallas_call | solution.py:1101

commit v5 on v4

--- a/solution.py
+++ b/solution.py
@@ -56,8 +56,7 @@
 def gelu_pair(values):
     half = jnp.exp2(values * values * (-0.5 * 1.4426950408889634))
     span = 1.0 + jnp.abs(values) * (0.3275911 * 0.7071067811865476)
-    guess = pl.reciprocal(span, approx=True)
-    t = guess * (2.0 - span * guess)
+    t = 1.0 / span
     poly = t * (
         0.5 * 0.254829592
         + t
@@ -357,7 +356,7 @@
         t.two_t[...] = r.two_low[...].T
 
     def columns(j):
-        return pl.ds(pl.multiple_of(j * chunk, chunk), chunk)
+        return slice(j * chunk, (j + 1) * chunk)
 
     def up_weight(j):
         return merged(r.w_up[:, :, :, :, columns(j)])
@@ -399,11 +398,8 @@
             there.active[:, cols], there.slope[:, cols] = active, slope
 
     def chunks(step):
-        def body(j, carry):
+        for j in range(shards):
             step(j)
-            return carry
-
-        lax.fori_loop(0, shards, body, 0)
 
     def last_norm(t):
         spreads = []

time: 195 us -> 185 us (0.949)
  Pallas kernels: 194 us -> 184 us
    pallas_call x2, Pallas kernels: 194 us -> 184 us  [run(): pl.pallas_call(functools.partial(kernel, (*ins, *outs, *scratch), constan...]
where the time goes in v5:
time: 185 us
  Pallas kernels  184 us (99%)
    pallas_call x2, Pallas kernels, run(): pl.pallas_call(functools.partial(kernel, (*ins, *outs, *scratch), constan...  184 us

profile of v5, /device:TPU:0, one launch (start us, length us, event | category | flops | bytes accessed | tf_op | source)
XLA Modules:
  0.0 184.8 jit_solution(9136886059497638556)
XLA Ops:
  0.7 177.0 %shard_map.358 = (f32[2560,512]{1,0:T(8,128)}, f32[40,128]{1,0:T(8,128)}, f32[32,1536]{1,0:T(8,128)}, f32[32,512]{1,0:T(8,128)}, f32[32,2048]{1,0:T(8,128)}, /*index=5*/f32[512,128]{1,0:T(8,128)}) custom-call(f32[2,26]{1,0:T(2,128)} %refs_0_.3, f32[2,26]{1,0:T(2,128)} %refs_1_.3, bf16[2560,512]{1,0:T(8,128)(2,1)} %refs_2_.1, bf16[18]{0:T(256)(128)(2,1)} %refs_3_.1, ...), custom_call_target="tpu_custom_call" | custom-call | flops 48318382080 | bytes 16777216 | tf_op jit(solution)/shard_map/pallas_call | solution.py:1097
  177.7 6.9 %shard_map.359 = (f32[1,1]{1,0:T(1,128)}, f32[2,26]{1,0:T(2,128)}, f32[32,64]{1,0:T(8,128)}, f32[32,1536]{1,0:T(8,128)}, f32[32,512]{1,0:T(8,128)}, /*index=5*/f...) custom-call(f32[2,26]{1,0:T(2,128)} %refs_0_.3, ...), custom_call_target="tpu_custom_call" | custom-call | bytes 16777216 | tf_op jit(solution)/shard_map/pallas_call | solution.py:1097

commit v6 on v5

--- a/solution.py
+++ b/solution.py
@@ -85,14 +85,12 @@
     return jnp.concatenate(blocks, 0)
 
 
-def gather_heads(blocks):
+def pair_products(left, right):
     lane = lax.broadcasted_iota(jnp.int32, (LENGTH, 2 * HEAD), 1)
     pairs = []
-    for pair in range(QUAD // 2):
-        lanes = slice(pair * 2 * HEAD, (pair + 1) * 2 * HEAD)
-        low = 2 * pair * HEAD
-        first, second = blocks[low : low + HEAD, lanes], blocks[low + HEAD : low + 2 * HEAD, lanes]
-        pairs.append(jnp.where(lane < HEAD, first, second))
+    for at in range(0, WIDE, 2 * HEAD):
+        block = dot(left[:, at : at + 2 * HEAD], right[:, at : at + 2 * HEAD], 0, 0)
+        pairs.append(jnp.where(lane < HEAD, block[0:HEAD], block[HEAD : 2 * HEAD]))
     return jnp.concatenate(pairs, 1)
 
 
@@ -131,8 +129,10 @@
         summed = jnp.sum(weights, 0, keepdims=True)
         probs.append((weights * (1.0 / summed)).astype(BF16))
         totals.append(highest + jnp.log(summed) * LOG2E)
-    blocks = [dot(prob, value, 0, 0) for prob, (_, _, value) in zip(probs, loaded, strict=True)]
-    done = [gather_heads(block).astype(BF16) for block in blocks]
+    done = [
+        pair_products(prob, value).astype(BF16)
+        for prob, (_, _, value) in zip(probs, loaded, strict=True)
+    ]
     for (seq, rows, (q, _, _)), result, total in zip(group, done, totals, strict=True):
         r.attended[rows, q] = result
         r.totals[pl.ds(seq, 1), q] = total
@@ -162,13 +162,13 @@
         value_grads = [dot(prob, above, 1, 0) for prob, above in zip(probs, aboves, strict=True)]
         key_grads = [dot(grad, query, 1, 0) for grad, query in zip(score_grads, queries, strict=True)]
         query_grads = [
-            dot(grad, r.qkv[rows, k], 0, 0)
+            pair_products(grad, r.qkv[rows, k])
             for (_, rows, (_, k, _)), grad in zip(group, score_grads, strict=True)
         ]
         for (_, rows, (q, k, v)), dq, dk, dv in zip(
             group, query_grads, key_grads, value_grads, strict=True
         ):
-            done.append((rows, q, (gather_heads(dq) * HEAD ** (-0.5)).astype(BF16)))
+            done.append((rows, q, (dq * HEAD ** (-0.5)).astype(BF16)))
             done.append((rows, k, (dk * HEAD ** (-0.5)).astype(BF16)))
             done.append((rows, v, dv.astype(BF16)))
     for rows, columns, grad in done:
@@ -771,20 +771,22 @@
             sc[z] = self.grad[z, :, 1 - p.c, :, self.cols].astype(self.kind)
             copy.start()
 
-    def start_x1(self):
+    def start_x1(self, pieces=range(4)):
         rc, p = self.buffers[1], self.place
-        for z, arrived, copy in zip(self.lines, self.c, self.x1, strict=True):
-            arrived.wait()
+        for k in pieces:
+            z = self.lines[k]
+            self.c[k].wait()
             away = self.grad[z, :, p.c, :, self.away].astype(F32)
             away += rc[z, :, :, self.local_away].astype(F32)
             self.sx1[z] = away.astype(self.kind)
-            copy.start()
+            self.x1[k].start()
             self.add((z, slice(None), p.c, slice(None), self.part), rc[z, :, :, self.local])
 
-    def start_y(self):
+    def start_y(self, pieces=range(4)):
         p = self.place
         held = self.buffers[5 if self.halved else 1]
-        for k, z in enumerate(self.lines):
+        for k in pieces:
+            z = self.lines[k]
             if self.halved:
                 self.x1[k].wait_recv()
             else:
@@ -795,16 +797,17 @@
             self.y[k].start()
             self.add((z, p.y, p.c, slice(None), self.part), held[z, p.y])
 
-    def start_z(self):
+    def start_z(self, pieces=range(4)):
         ry, p = self.buffers[2], self.place
-        for k in range(3):
-            owner = self.lines[k + 1]
-            self.y[k + 1].wait_recv()
+        for k in pieces:
+            owner = self.lines[k]
+            self.y[k].wait_recv()
+            if k == 0:
+                self.add((owner, p.y, p.c, slice(None), self.part), ry[owner])
+                continue
             away = self.grad[owner, p.y, p.c, :, self.part].astype(F32) + ry[owner].astype(F32)
-            self.sz[k][...] = away.astype(self.kind)
-            self.z[k].start()
-        self.y[0].wait_recv()
-        self.add((p.z, p.y, p.c, slice(None), self.part), ry[p.z])
+            self.sz[k - 1][...] = away.astype(self.kind)
+            self.z[k - 1].start()
 
     def start_x(self):
         rz, p = self.buffers[3], self.place
@@ -916,6 +919,8 @@
     pack.start_y()
     q.start_y()
     pack.start_c()
+    for group in (out, up0, up1, down0, down1):
+        group.start_z()
     frame_values(r)
     k.start_y()
     pack.ready()
@@ -926,8 +931,6 @@
     norm_pass(r)
     k.start_c()
     v.start_c()
-    for group in (out, up0, up1, down0, down1):
-        group.start_z()
     q.ready()
     project_third(r, 0)
     clear(r)
@@ -972,23 +975,26 @@
         lambda i: at_step(
             i,
             {
-                1: [down.start_y, up.start_x1],
-                2: [out.start_x1],
-                6: [down.start_z, up.start_y],
-                7: [out.start_y],
-                9: [up.start_z],
+                1: [down.start_y],
+                2: [up.start_x1],
+                3: [out.start_x1],
+                7: [lambda: up.start_y([0])],
+                9: [lambda: down.start_z([0, 1]), lambda: up.start_y([1])],
             },
         ),
     )
     qkv_weight_grad(r, 0)
     q.start_c()
+    down.start_z([2])
+    up.start_y([2])
     qkv_weight_grad(r, 2)
     v.start_c()
     q.start_y()
+    down.start_z([3])
+    up.start_y([3])
     qkv_weight_grad(r, 1)
     k.start_c()
     v.start_x1()
-    out.start_z()
     k.start_y()
 
     def stored(i):
@@ -1002,27 +1008,33 @@
         lambda i: at_step(
             i,
             {
-                2: [down.start_x],
-                3: [up.start_x, q.start_z],
-                5: [v.start_y, out.start_x],
-                6: [k.start_z],
-                8: [v.start_z, q.start_x],
+                1: [out.start_y],
+                3: [up.start_z],
+                4: [v.start_y],
+                5: [q.start_z],
+                6: [out.start_z],
+                8: [down.start_x],
+                9: [k.start_z],
             },
         ),
         lambda i: stored(i).start(),
     )
     pack_grads(r)
     pack.start_c()
+    v.start_z()
+    q.start_x()
+    pack.start_y()
+    up.start_x()
+    out.start_x()
     k.start_x()
+    pack.start_z()
     v.start_x()
-    pack.start_y()
     down.finish(r.down_out)
+    pack.start_x()
     up.finish(r.up_out)
-    pack.start_z()
     out.finish(r.out_out)
     for group in (q, k, v):
         group.finish(r.qkv_out)
-    pack.start_x()
     for i in range(r.middle_grad.shape[0] // (4 * LENGTH)):
         stored(i).wait()
     for group in gathers + reduces:

time: 185 us -> 186 us (level)
  no operation moved by 1% of the time
where the time goes in v6:
time: 186 us
  Pallas kernels  185 us (99%)
    pallas_call x2, Pallas kernels, run(): pl.pallas_call(functools.partial(kernel, (*ins, *outs, *scratch), constan...  185 us

profile of v6, /device:TPU:0, one launch (start us, length us, event | category | flops | bytes accessed | tf_op | source)
XLA Modules:
  0.0 185.6 jit_solution(6189112203812759413)
XLA Ops:
  0.7 177.9 %shard_map.358 = (f32[2560,512]{1,0:T(8,128)}, f32[40,128]{1,0:T(8,128)}, f32[32,1536]{1,0:T(8,128)}, f32[32,512]{1,0:T(8,128)}, f32[32,2048]{1,0:T(8,128)}, /*index=5*/f32[512,128]{1,0:T(8,128)}) custom-call(f32[2,26]{1,0:T(2,128)} %refs_0_.3, f32[2,26]{1,0:T(2,128)} %refs_1_.3, bf16[2560,512]{1,0:T(8,128)(2,1)} %refs_2_.1, bf16[18]{0:T(256)(128)(2,1)} %refs_3_.1, ...), custom_call_target="tpu_custom_call" | custom-call | flops 48318382080 | bytes 16777216 | tf_op jit(solution)/shard_map/pallas_call | solution.py:1109
  178.6 6.9 %shard_map.359 = (f32[1,1]{1,0:T(1,128)}, f32[2,26]{1,0:T(2,128)}, f32[32,64]{1,0:T(8,128)}, f32[32,1536]{1,0:T(8,128)}, f32[32,512]{1,0:T(8,128)}, /*index=5*/f...) custom-call(f32[2,26]{1,0:T(2,128)} %refs_0_.3, ...), custom_call_target="tpu_custom_call" | custom-call | bytes 16777216 | tf_op jit(solution)/shard_map/pallas_call | solution.py:1109

commit v7 on v6

--- a/solution.py
+++ b/solution.py
@@ -382,14 +382,13 @@
         for at in range(0, rows, THIN):
             strip = slice(at, at + THIN)
             part = (above[strip] * here.slope[strip, cols].astype(F32)).astype(BF16)
-            r.hidden_grad[strip, :] = part
+            here.slope[strip, cols] = part
             total += fold_rows(part.astype(F32))
         add_columns(r.g_down.at[j], dot(r.low_t[...], here.active[:, cols], 1, 0))
-        r.two_in[...] += dot(r.hidden_grad[...], up_weight(j), 1, 1)
         add_grad(
             r.g_up,
             (everything, everything, everything, everything, cols),
-            dot(here.two_t[...], r.hidden_grad[...], 1, 0),
+            dot(here.two_t[...], here.slope[:, cols], 1, 0),
         )
         r.g_up_bias[:, cols] = total
         if there is not None:
@@ -440,7 +439,6 @@
         for k, total in zip((GL, BL, DB), sums, strict=True):
             r.g_small[k] = total
         r.low_t[...] = r.low[...].T
-        r.two_in[...] = jnp.zeros((rows, width), F32)
 
     def two_norm_back(t):
         sums = [r.g_small[k] for k in (G2, B2)]
@@ -485,6 +483,7 @@
         if not last:
             before(there, *ahead)
         chunks(lambda j: both_ways(j, here, None if last else there))
+        r.two_in[...] = dot(here.slope[...], merged(r.w_up[...]), 1, 1)
 
     before(sides[0], *begin(0))
     arrive()
@@ -546,7 +545,7 @@
         r.g_positions[...] = jnp.concatenate(frames, 0)
         for k, total in zip((G1, B1), sums, strict=True):
             r.g_small[k] = total
-        r.middle_grad[pl.ds(row, rows), :] = jnp.concatenate(grads, 0)
+        r.attended[pl.ds(row, rows), :] = jnp.concatenate(grads, 0).astype(BF16)
         tile_done(i)
         return carry
 
@@ -674,19 +673,20 @@
         self.full, self.own, self.part, self.place, self.halved = full, own, part, place, halved
         mine = full.at[p.z, p.y, p.c, :, part]
         self.z = [copy(own.at[:, part], mine, k, p.at(z=p.z_partner(k))) for k in range(3)]
-        self.y, self.x, self.near, self.far = [], [], [], []
+        self.y, self.x, self.near, self.far, self.swapped = [], [], [], [], []
+        sibling = p.at(c=1 - p.c)
         for k, z in enumerate(p.lines()):
             shard = full.at[z, p.y, p.c, :, part]
             self.y.append(copy(shard, shard, 3 + k, p.at(y=1 - p.y)))
+            self.near.append(copy(shard, shard, 7 + k, sibling))
+            shard = full.at[z, 1 - p.y, p.c, :, part]
+            self.far.append(copy(shard, shard, 11 + k, sibling))
             if halved:
                 pair = full.at[z, :, p.c, :, part]
-                self.x.append(copy(pair, pair, 7 + k, p.at(x=1 - p.x)))
-                pair = full.at[z, :, p.c, :, cols]
-                self.far.append(copy(pair, pair, 11 + k, p.at(c=1 - p.c)))
-            else:
-                self.near.append(copy(shard, shard, 7 + k, p.at(c=1 - p.c)))
-                shard = full.at[z, 1 - p.y, p.c, :, part]
-                self.far.append(copy(shard, shard, 11 + k, p.at(c=1 - p.c)))
+                self.x.append(copy(pair, pair, 15 + k, p.at(x=1 - p.x)))
+                other = pl.ds(pl.multiple_of(at + (1 - p.x) * (count // 2), 128), count // 2)
+                pair = full.at[z, :, p.c, :, other]
+                self.swapped.append(copy(pair, pair, 19 + k, sibling))
 
     def start_z(self):
         for copy in self.z:
@@ -694,32 +694,32 @@
         p = self.place
         self.full[p.z, p.y, p.c, :, self.part] = self.own[:, self.part]
         self.y[0].start()
-        if not self.halved:
-            self.near[0].start()
+        self.near[0].start()
 
     def start_y(self):
         for k, copy in enumerate(self.z):
             copy.wait_recv()
             self.y[k + 1].start()
-            if not self.halved:
-                self.near[k + 1].start()
+            self.near[k + 1].start()
 
     def start_x(self):
-        for arrived, copy in zip(self.y, self.x, strict=True):
+        for arrived, copy, far in zip(self.y, self.x, self.far, strict=True):
             arrived.wait_recv()
             copy.start()
+            far.start()
 
     def start_c(self):
-        for arrived, copy in zip(self.x if self.halved else self.y, self.far, strict=True):
+        pairs = zip(self.x, self.swapped) if self.halved else zip(self.y, self.far)
+        for arrived, copy in pairs:
             arrived.wait_recv()
             copy.start()
 
     def ready(self):
-        for copy in self.near + self.far:
+        for copy in self.near + self.far + self.swapped:
             copy.wait_recv()
 
     def close(self):
-        for copy in self.z + self.y + self.x + self.near + self.far:
+        for copy in self.z + self.y + self.x + self.near + self.far + self.swapped:
             copy.wait_send()
 
 
@@ -1000,7 +1000,7 @@
     def stored(i):
         rows = pl.ds(pl.multiple_of(i * 4 * LENGTH, 4 * LENGTH), 4 * LENGTH)
         return pltpu.make_async_copy(
-            r.middle_grad.at[rows, :], r.tokens_grad.at[rows, :], r.store_sem.at[i]
+            r.attended.at[rows, :], r.tokens_grad.at[rows, :], r.store_sem.at[i]
         )
 
     start_back(
@@ -1051,7 +1051,7 @@
         for k, part in enumerate(parts)
     ]
     stores = [
-        pltpu.make_async_copy(r.held.at[part, :], r.o_tokens.at[part, :], r.store_sem.at[k])
+        pltpu.make_async_copy(r.wide.at[part, :], r.o_tokens.at[part, :], r.store_sem.at[k])
         for k, part in enumerate(parts)
     ]
     for load in loads:
@@ -1073,8 +1073,9 @@
     r.o_actor_bias[...] = turned[BIAS_AT : BIAS_AT + 1, :].reshape(part)[0:slots]
     r.o_loss[...] = features[0:1, LOSS_AT : LOSS_AT + 1] * (1.0 / count)
     r.o_up_bias[...] = r.pack[part : part + 1, :].reshape(128)
-    for load, store in zip(loads, stores, strict=True):
+    for part, load, store in zip(parts, loads, stores, strict=True):
         load.wait()
+        r.wide[part, :] = r.held[part, :].astype(F32)
         store.start()
     for store in stores:
         store.wait()
@@ -1096,7 +1097,7 @@
     for third in range(3):
         qkv_weight_grad(r, third)
     start_back(r, lambda i: None, lambda i: None)
-    store = pltpu.make_async_copy(r.middle_grad, r.tokens_grad, r.local_sem.at[1])
+    store = pltpu.make_async_copy(r.attended, r.tokens_grad, r.local_sem.at[1])
     store.start()
     store.wait()
 
@@ -1197,7 +1198,7 @@
             down_out=((width, hidden_part), F32),
         )
         outs = dict(
-            tokens_grad=((row_count, width), F32), pack_out=((PACK_GRAD_ROWS, 128), F32)
+            tokens_grad=((row_count, width), BF16), pack_out=((PACK_GRAD_ROWS, 128), F32)
         )
         scratch |= grads | weight_shapes
         scratch |= dict(
@@ -1208,8 +1209,8 @@
             small=((8, width), F32),
             actor=((SLOTS, width), BF16),
             up_bias=((1, hidden_width), F32),
-            gather_send=pltpu.SemaphoreType.DMA((GATHERS, 15)),
-            gather_recv=pltpu.SemaphoreType.DMA((GATHERS, 15)),
+            gather_send=pltpu.SemaphoreType.DMA((GATHERS, 23)),
+            gather_recv=pltpu.SemaphoreType.DMA((GATHERS, 23)),
             reduce_send=pltpu.SemaphoreType.DMA((len(REDUCES), 16)),
             reduce_recv=pltpu.SemaphoreType.DMA((len(REDUCES), 16)),
             store_sem=pltpu.SemaphoreType.DMA((row_count // (4 * LENGTH),)),
@@ -1241,7 +1242,12 @@
             stats
             | dict(pack=pack, qkv=qkv_g, out=out_g, up=up_g, down=down_g, tokens=tokens_grad),
             final | dict.fromkeys(vectors, vector),
-            dict(held=((row_count, width), F32), load_sem=copies, store_sem=copies),
+            dict(
+                held=((row_count, width), BF16),
+                wide=((row_count, width), F32),
+                load_sem=copies,
+                store_sem=copies,
+            ),
         )
         loss, new_stats, pos_g, qkv_g, out_g, up_g, down_g = done[:7]
         up_bias_g, actor_g, actor_bias_g, tokens_grad = done[7:11]
@@ -1284,7 +1290,7 @@
         actor=jnp.pad(packed[7 : 7 + slots], ((0, SLOTS - slots), (0, 0))),
         up_bias=gather(up_bias, 0).astype(F32).reshape(1, hidden_width),
     )
-    outs = dict(tokens_grad=((row_count, width), F32)) | grads
+    outs = dict(tokens_grad=((row_count, width), BF16)) | grads
     tokens_grad, *sums = run(local_kernel, scale, ins, outs, scratch, flops)
     sums = Names(grads, sums)
 
@@ -1304,7 +1310,7 @@
     return (
         head_total[SLOTS] / token_total,
         DECAY_RATE * running + (1.0 - DECAY_RATE) * percentiles,
-        tokens_grad,
+        tokens_grad.astype(F32),
         side[7 + slots :],
         side[G1],
         side[B1],

time: 186 us -> 186 us (level)
  no operation moved by 1% of the time
where the time goes in v7:
time: 186 us
  Pallas kernels  185 us (99%)
    pallas_call x2, Pallas kernels, run(): pl.pallas_call(functools.partial(kernel, (*ins, *outs, *scratch), constan...  185 us

profile of v7, /device:TPU:0, one launch (start us, length us, event | category | flops | bytes accessed | tf_op | source)
XLA Modules:
  0.0 186.3 jit_solution(15784760528547027851)
XLA Ops:
  0.7 179.8 %shard_map.358 = (bf16[2560,512]{1,0:T(8,128)(2,1)}, f32[40,128]{1,0:T(8,128)}, f32[32,1536]{1,0:T(8,128)}, f32[32,512]{1,0:T(8,128)}, f32[32,2048]{1,0:T(8,128)}, /*index=5*/f32[512,128]{1,0:T(8,128)}) custom-call(f32[2,26]{1,0:T(2,128)} %refs_0_.3, f32[2,26]{1,0:T(2,128)} %refs_1_.3, bf16[2560,512]{1,0:T(8,128)(2,1)} %refs_2_.1, bf16[18]{0:T(256)(128)(2,1)} %refs_3_.1, ...), custom_call_target="tpu_custom_call" | custom-call | flops 48318382080 | bytes 16777216 | tf_op jit(solution)/shard_map/pallas_call | solution.py:1110
  180.5 5.6 %shard_map.359 = (f32[1,1]{1,0:T(1,128)}, f32[2,26]{1,0:T(2,128)}, f32[32,64]{1,0:T(8,128)}, f32[32,1536]{1,0:T(8,128)}, f32[32,512]{1,0:T(8,128)}, /*index=5*/f...) custom-call(f32[2,26]{1,0:T(2,128)} %refs_0_.3, ...), custom_call_target="tpu_custom_call" | custom-call | bytes 16777216 | tf_op jit(solution)/shard_map/pallas_call | solution.py:1110
